TPU v7x, 512 devices: a whole 4x8x8 slice. The times are simulated.
512 devices in a mesh: tgt: 32 (over z, x), src: 16 (over y, core).
Axes of the slice: x: 4, y: 8, z: 8, core: 2. Of those that a mesh axis runs over, the one named last changes fastest.
Arguments:
- src_emb: bfloat16 [16384, 300], P('src'), may hold values from -4 to 4
- tgt_emb: bfloat16 [131072, 300], P('tgt'), may hold values from -5 to 5
- g_init: float32 [131072], P('tgt'), may hold values from -1 to 1
- log_src: float32 [16384], P('src'), may hold values from -2 to 2
- log_tgt: float32 [131072], P('tgt'), may hold values from -2 to 2
- cand_ids: int32 [32, 128], P('src'), may hold values from 0 to 255, as said below
- cand_count: int32 [32], P('src'), may hold values from 8 to 128, as said below
Outputs:
- row_potential: float32 [16384], P('src')
- col_potential: float32 [131072], P('tgt')
- mapped: bfloat16 [16384, 300], P('src')
- row_mass: float32 [16384], P('src')
Inputs may be any that keep to these rules, and one draw needn't show every extreme that they name: `cand_ids`: target block ids; every target block is a live candidate of some source block; slots at or past the count are ignored. `cand_count`: live slots of a source block.
All inputs are finite; a program needn't handle non-finite values.
Results may differ from a plain program's by a relative error of at most 0.0045.
Values may be sent and summed in bfloat16 or wider, within the bound.
No kernel may reach another device: no remote copies, remote signals or barrier semaphores. Data moves between devices by JAX's collectives and lax.ppermute only.
A program may use at most 128 MiB of HBM per device.

v0:
```python
import jax
import jax.numpy as jnp
from jax import lax
from jax.sharding import PartitionSpec as P

BLOCK = 512


EPS = 0.2
NEG = -1e30


def combined_all(array, axis, combine):
    everything = jax.tree.map(lambda part: lax.all_gather(part, axis), array)
    first = jax.tree.map(lambda part: part[0], everything)

    def turn(k, so_far):
        return combine(so_far, jax.tree.map(lambda part: part[k], everything))

    return lax.fori_loop(1, lax.axis_size(axis), turn, first)


def combine_lse(first, second):
    peak = jnp.maximum(first[0], second[0])
    total = first[1] * jnp.exp(first[0] - peak) + second[1] * jnp.exp(second[0] - peak)
    return (peak, total)


def masked_stats(values, mask, axis):
    peak = jnp.max(values, axis=axis)
    total = jnp.sum(jnp.where(mask, jnp.exp(values - jnp.expand_dims(peak, axis)), 0.0), axis=axis)
    return (peak, total)


def local(src_emb, tgt_emb, g_init, log_src, log_tgt, cand_ids, cand_count):
    s_rows = src_emb.shape[0]
    t_cols = tgt_emb.shape[0]
    src_blocks = s_rows // BLOCK
    tgt_blocks = t_cols // BLOCK
    slots = cand_ids.shape[1]
    owned = lax.axis_index("tgt") * tgt_blocks + jnp.arange(tgt_blocks, dtype=jnp.int32)
    live = jnp.arange(slots, dtype=jnp.int32)[None, :] < cand_count[:, None]
    tile_mask = jnp.any((cand_ids[:, :, None] == owned[None, None, :]) & live[:, :, None], axis=1)
    contract = (((1,), (1,)), ((), ()))
    mask = jnp.broadcast_to(
        tile_mask[:, None, :, None], (src_blocks, BLOCK, tgt_blocks, BLOCK)
    ).reshape(s_rows, t_cols)
    scores = lax.dot_general(src_emb, tgt_emb, contract, preferred_element_type=jnp.float32)
    z_vals = jnp.where(mask, (g_init[None, :] + scores) / EPS, NEG)
    peak, total = masked_stats(z_vals, mask, 1)
    peak_all, total_all = combined_all((peak, total), "tgt", combine_lse)
    row_potential = EPS * log_src - EPS * (peak_all + jnp.log(total_all))
    y_vals = jnp.where(mask, (row_potential[:, None] + scores) / EPS, NEG)
    cpeak, ctotal = masked_stats(y_vals, mask, 0)
    cpeak, ctotal = combined_all((cpeak, ctotal), "src", combine_lse)
    col_potential = EPS * log_tgt - EPS * (cpeak + jnp.log(ctotal))
    q_vals = jnp.where(mask, (col_potential[None, :] + scores) / EPS, NEG)
    local_top = jnp.max(q_vals, axis=1)
    row_top = lax.pmax(local_top, "tgt")
    weights = jnp.where(mask, jnp.exp(q_vals - row_top[:, None]), 0.0).astype(jnp.bfloat16)
    numer = jnp.dot(weights, tgt_emb, preferred_element_type=jnp.float32)
    denom = jnp.sum(weights, axis=1, dtype=jnp.float32)
    numer_all, denom_all = lax.psum((numer, denom), "tgt")
    mapped = (numer_all / denom_all[:, None]).astype(jnp.bfloat16)
    row_mass = row_potential / EPS + row_top + jnp.log(denom_all)
    return (row_potential, col_potential, mapped, row_mass)


def solution(mesh):
    return jax.shard_map(
        local,
        mesh=mesh,
        in_specs=(
            P("src", None),
            P("tgt", None),
            P("tgt"),
            P("src"),
            P("tgt"),
            P("src", None),
            P("src"),
        ),
        out_specs=(P("src"), P("tgt"), P("src", None), P("src")),
        check_vma=False,
    )
```

profile of v0, /device:TPU:1, one launch (start us, length us, event | category | flops | bytes accessed | tf_op | source)
XLA Modules:
  0.0 442.9 jit_solution(17325340615585305550)
XLA Ops:
  7.2 0.9 iota_compare_fusion
  8.1 0.9 and_reduce_fusion
  9.0 1.2 broadcast_in_dim.13
  10.1 4.3 copy.11
  14.5 11.5 %fusion = (f32[1024]{0:T(1024)S(1)}, f32[1024,4096]{1,0:T(8,128)}) fusion(pred[1024,4096]{1,0:T(8,128)(4,1)S(1)} %bitcast.19, f32[4096]{0:T(1024)} %param.13, bf16[1024,300]{0,1:T(8,128)(2,1)} %param.11, bf16[4096,300]{0,1:T(8,128)(2,1)S(1)} %copy-done), kind=kOutput, calls=%fused_computation.13 | convolution fusion | flops 2533358592 | bytes 24064000 | tf_op jit(solution)/shard_map/dot_general | solution.py:48
  26.0 40.2 %all-gather = f32[32768]{0:T(1024)S(1)} all-gather(f32[1024]{0:T(1024)S(1)} %get-tuple-element.304), channel_id=2, replica_groups=mesh['tgt'=32,'src'=16] {'tgt'}, dimensions={0}, use_global_device_ids=true | all-gather | bytes 135168 | tf_op jit(solution)/shard_map/all_gather | solution.py:14
  66.2 9.9 %select_reduce_fusion.1 = f32[1024]{0:T(1024)S(1)} fusion(pred[1024,4096]{1,0:T(8,128)(4,1)} %bitcast.20, f32[1024,4096]{1,0:T(8,128)} %get-tuple-element.305, f32[1024]{0:T(1024)S(1)} %get-tuple-element.304, f32[4096]{0:T(1024)S(1)} %copy-done.5), kind=kLoop, calls=%fused_computation.11 | loop fusion | flops 25164800 | bytes 20996096 | tf_op jit(solution)/shard_map/reduce_sum | solution.py:31
  76.0 32.5 %all-gather.1 = f32[32768]{0:T(1024)S(1)} all-gather(f32[1024]{0:T(1024)S(1)} %select_reduce_fusion.1), channel_id=3, replica_groups=mesh['tgt'=32,'src'=16] {'tgt'}, dimensions={0}, use_global_device_ids=true | all-gather | bytes 135168 | tf_op jit(solution)/shard_map/all_gather | solution.py:14
  108.6 1.8 while.34
  110.5 10.9 %fusion.1 = f32[4096]{0:T(1024)S(1)} fusion(pred[1024,4096]{1,0:T(8,128)(4,1)} %bitcast.21, f32[1024,4096]{1,0:T(8,128)} %get-tuple-element.305, f32[1024]{0:T(1024)S(1)} %multiply_subtract_fusion.1), kind=kLoop, calls=%fused_computation.14 | loop fusion | flops 16773120 | bytes 20992000 | tf_op jit(solution)/shard_map/reduce_max | solution.py:30
  121.4 9.7 %select_reduce_fusion = f32[4096]{0:T(1024)S(1)} fusion(pred[1024,4096]{1,0:T(8,128)(4,1)} %bitcast.22, f32[1024,4096]{1,0:T(8,128)} %get-tuple-element.305, f32[4096]{0:T(1024)S(1)} %fusion.1, f32[1024]{0:T(1024)S(1)} %multiply_subtract_fusion.1), kind=kLoop, calls=%fused_computation.9 | loop fusion | flops 25161728 | bytes 21008384 | tf_op jit(solution)/shard_map/reduce_sum | solution.py:31
  131.1 38.9 %all-gather.2 = f32[65536]{0:T(1024)S(1)} all-gather(f32[4096]{0:T(1024)S(1)} %fusion.1), channel_id=4, replica_groups=mesh['tgt'=32,'src'=16] {'src'}, dimensions={0}, use_global_device_ids=true | all-gather | bytes 278528 | tf_op jit(solution)/shard_map/all_gather | solution.py:14
  170.0 0.1 reshape.48
  170.1 15.6 %all-gather.3 = f32[65536]{0:T(1024)S(1)} all-gather(f32[4096]{0:T(1024)S(1)} %select_reduce_fusion), channel_id=5, replica_groups=mesh['tgt'=32,'src'=16] {'src'}, dimensions={0}, use_global_device_ids=true | all-gather | bytes 278528 | tf_op jit(solution)/shard_map/all_gather | solution.py:14
  185.8 0.1 reshape.49
  185.8 1.3 while.35
  187.1 10.4 %fusion.2 = f32[1024]{0:T(1024)S(1)} fusion(pred[1024,4096]{1,0:T(8,128)(4,1)} %bitcast.23, f32[1024,4096]{1,0:T(8,128)} %get-tuple-element.305, f32[4096]{0:T(1024)S(1)} %multiply_subtract_fusion), kind=kLoop, calls=%fused_computation.15 | loop fusion | flops 16776192 | bytes 20992000 | tf_op jit(solution)/shard_map/reduce_max | solution.py:58
  197.5 58.6 %pmax.7 = f32[1024]{0:T(1024)S(1)} all-reduce(f32[1024]{0:T(1024)S(1)} %fusion.2), channel_id=1, replica_groups=mesh['tgt'=32,'src'=16] {'tgt'}, use_global_device_ids=true, to_apply=%region_10.11 | all-reduce | flops 1024 | bytes 8192 | tf_op jit(solution)/shard_map/pmax | solution.py:59
  256.1 10.5 %convert_reduce_fusion = (f32[1024]{0:T(1024)S(1)}, bf16[1024,4096]{1,0:T(8,128)(2,1)S(1)}) fusion(pred[1024,4096]{1,0:T(8,128)(4,1)} %bitcast.24, f32[1024]{0:T(1024)S(1)} %pmax.7, f32[1024,4096]{1,0:T(8,128)} %get-tuple-element.305, f32[4096]{0:T(1024)S(1)} %multiply_subtract_fusion), kind=kLoop, calls=%fused_computation.6 | loop fusion | flops 33553408 | bytes 29384704 | tf_op jit(solution)/shard_map/reduce_sum | solution.py:62
  266.7 4.0 fusion.3
  270.7 56.2 %psum.15 = f32[1024]{0:T(1024)S(1)} all-reduce(f32[1024]{0:T(1024)S(1)} %get-tuple-element.298), channel_id=1, replica_groups=mesh['tgt'=32,'src'=16] {'tgt'}, use_global_device_ids=true, to_apply=%region_13.14 | all-reduce | flops 1024 | bytes 8192 | tf_op jit(solution)/shard_map/psum | solution.py:63
  326.9 0.6 log_add_fusion
  327.5 106.4 %all-reduce.2.cloned.1.call-done = f32[1024,300]{0,1:T(8,128)} async-done(((f32[1024,300]{0,1:T(8,128)}), f32[1024,300]{0,1:T(8,128)}) %all-reduce.2.cloned.1.call-update) | async-done | bytes 1228816 | tf_op jit(solution)/shard_map/psum | solution.py:63
  433.8 2.2 divide_convert_fusion
  (117 shorter events, 1.8 us)
Async XLA Ops:
  7.2 7.3 %copy-start = (bf16[4096,300]{0,1:T(8,128)(2,1)S(1)}, bf16[4096,300]{0,1:T(8,128)(2,1)}, u32[]{:S(2)}) copy-start(bf16[4096,300]{0,1:T(8,128)(2,1)} %param.12) | copy-start | bytes 7372804
  7.2 426.7 %all-reduce.2.cloned.1.call-start = ((), (), s32[]{:S(2)}) async-start(), calls=%async_computation | async-start | bytes 2490368 | tf_op jit(solution)/shard_map/psum | solution.py:63
  14.4 11.5 %copy-start.1 = (pred[128,8,8,512]{3,1,2,0:T(8,128)(4,1)}, pred[128,8,8,512]{3,1,2,0:T(8,128)(4,1)S(1)}, u32[]{:S(2)}) copy-start(pred[128,8,8,512]{3,1,2,0:T(8,128)(4,1)S(1)} %copy.11) | copy-start | bytes 12582916
  14.5 51.7 %copy-start.5 = (f32[4096]{0:T(1024)S(1)}, f32[4096]{0:T(1024)}, u32[]{:S(2)}) copy-start(f32[4096]{0:T(1024)} %param.13) | copy-start | bytes 49156
  26.0 84.5 %copy-start.6 = (f32[1024]{0:T(1024)S(1)}, f32[1024]{0:T(1024)}, u32[]{:S(2)}) copy-start(f32[1024]{0:T(1024)} %param.14) | copy-start | bytes 12292
  110.4 216.4 %copy-start.3 = (f32[1024]{0:T(1024)}, f32[1024]{0:T(1024)S(1)}, u32[]{:S(2)}) copy-start(f32[1024]{0:T(1024)S(1)} %multiply_subtract_fusion.1) | copy-start | bytes 12292
  121.4 65.7 %copy-start.4 = (f32[4096]{0:T(1024)S(1)}, f32[4096]{0:T(1024)}, u32[]{:S(2)}) copy-start(f32[4096]{0:T(1024)} %param.15) | copy-start | bytes 49156
  187.1 79.6 %copy-start.2 = (f32[4096]{0:T(1024)}, f32[4096]{0:T(1024)S(1)}, u32[]{:S(2)}) copy-start(f32[4096]{0:T(1024)S(1)} %multiply_subtract_fusion) | copy-start | bytes 49156
Sparse Core Ops, SparseCore 0:
  270.8 162.9 all-reduce.1
where the time goes:
time: 447 us; the launch traced here: 443 us
  blocking collectives  242 us (54%)
  waiting for transfers between devices  106 us (24%)
  other arithmetic  56.7 us (13%)
  matrix products  15.5 us (3%)
  between operations  14.2 us (3%)
  local copies, waits for them, and re-layouts  6.58 us (1%)
    all_gather x4, blocking collectives, combined_all(): everything = jax.tree.map(lambda part: lax.all_gather(part, axis), array)  127 us
    psum x1, waiting for transfers between devices, local(): numer_all, denom_all = lax.psum((numer, denom), 'tgt')  106 us
    pmax x1, blocking collectives, local(): row_top = lax.pmax(local_top, 'tgt')  58.6 us
    psum x1, blocking collectives, local(): numer_all, denom_all = lax.psum((numer, denom), 'tgt')  56.2 us
    reduce_sum x2, other arithmetic, masked_stats(): jnp.sum(jnp.where(mask, jnp.exp(values - jnp.expand_dims(peak, axis)), 0....  19.6 us
    dot_general x1, matrix products, local(): lax.dot_general(src_emb, tgt_emb, contract, preferred_element_type=jnp.fl...  11.5 us
    reduce_max x1, other arithmetic, masked_stats(): peak = jnp.max(values, axis=axis)  10.9 us
    reduce_sum x1, other arithmetic, local(): denom = jnp.sum(weights, axis=1, dtype=jnp.float32)  10.5 us
  transfers between devices with their start and end apart: 1, of which 1 were waited for; matrix products, arithmetic and copies ran while one was open for 0% of the time, Pallas kernels for 0%

commit v1 on v0

v1 whole, which is shorter than its diff:
```python
import functools

import jax
import jax.numpy as jnp
from jax import lax
from jax.experimental import pallas as pl
from jax.experimental.pallas import tpu as pltpu
from jax.sharding import PartitionSpec as P

BLOCK = 512
LANES = 128
EPS = 0.2
INV = 5.0
NEG = -1e30
GROUPS = 4
CHUNK = 80
NT = (((1,), (1,)), ((), ()))
F32 = jnp.float32
BF16 = jnp.bfloat16


def logsum(values, axis):
    peak = jnp.max(values, axis=axis, keepdims=True)
    return peak + jnp.log(jnp.sum(jnp.exp(values - peak), axis=axis, keepdims=True))


def safe_log(peak, total):
    return jnp.where(total > 0.0, peak + jnp.log(jnp.where(total > 0.0, total, 1.0)), NEG)


def lane_parts(tile):
    return [tile[:, k * LANES : (k + 1) * LANES] for k in range(tile.shape[1] // LANES)]


def three_parts(value):
    high = value.astype(BF16).astype(F32)
    rest = value - high
    middle = rest.astype(BF16).astype(F32)
    return high, middle, rest - middle


def tiles(live_ref, body):
    blocks, columns = live_ref.shape

    def step(i, carry):
        b, t = i // columns, i % columns

        @pl.when(live_ref[b, t] > 0)
        def _():
            body(b, t)

        return carry

    lax.fori_loop(0, blocks * columns, step, 0)


def score(rows_ref, tgt_ref, b, t):
    rows = rows_ref[pl.ds(pl.multiple_of(b * BLOCK, BLOCK), BLOCK), :]
    cols = tgt_ref[:, pl.ds(pl.multiple_of(t * BLOCK, BLOCK), BLOCK)]
    return jnp.dot(rows[:, : cols.shape[0]], cols, preferred_element_type=F32)


def row_kernel(live_ref, src_ref, tgt_ref, g_ref, rows_ref, out_ref, pad, peak, total, packed):
    width, s_rows = src_ref.shape
    pad[...] = jnp.zeros_like(pad)
    pad[:width, :] = src_ref[...].astype(F32)
    for k in range(s_rows // LANES):
        piece = pad[:, k * LANES : (k + 1) * LANES]
        rows_ref[k * LANES : (k + 1) * LANES, :] = piece.T.astype(BF16)
    peak[...] = jnp.full_like(peak, NEG)
    total[...] = jnp.zeros_like(total)

    def body(b, t):
        g = g_ref[:, pl.ds(pl.multiple_of(t * BLOCK, BLOCK), BLOCK)] * INV
        z = lane_parts(score(rows_ref, tgt_ref, b, t) * INV + g)
        old = peak[b]
        new = functools.reduce(jnp.maximum, z, old)
        peak[b] = new
        total[b] = total[b] * jnp.exp(old - new) + sum(jnp.exp(part - new) for part in z)

    tiles(live_ref, body)
    per_block = BLOCK // LANES
    for b in range(s_rows // BLOCK):
        turned = peak[b].T
        top = jnp.max(turned, axis=0, keepdims=True)
        mass = jnp.sum(total[b].T * jnp.exp(turned - top), axis=0, keepdims=True)
        for k, part in enumerate(lane_parts(safe_log(top, mass))):
            packed[b * per_block + k : b * per_block + k + 1, :] = part
    out_ref[...] = jnp.broadcast_to(packed[...][None], out_ref.shape)


def col_kernel(live_ref, rows_ref, tgt_ref, lse_ref, log_ref, f_ref, out_ref, fcol, peak, total, packed):
    f = EPS * log_ref[...] - EPS * logsum(lse_ref[...], 0)[0]
    f_ref[...] = f
    for k in range(f.shape[0]):
        row = jnp.broadcast_to(f[k : k + 1, :] * INV, (LANES, LANES))
        fcol[k * LANES : (k + 1) * LANES, :] = row.T
    peak[...] = jnp.full_like(peak, NEG)
    total[...] = jnp.zeros_like(total)

    def body(b, t):
        own = fcol[pl.ds(pl.multiple_of(b * BLOCK, BLOCK), BLOCK), :]
        y = score(rows_ref, tgt_ref, b, t) * INV + jnp.concatenate([own] * (BLOCK // LANES), axis=1)
        y = y.reshape(BLOCK // 8, 8, BLOCK)
        old = peak[t]
        new = jnp.maximum(old, jnp.max(y, axis=0))
        peak[t] = new
        total[t] = total[t] * jnp.exp(old - new) + jnp.sum(jnp.exp(y - new[None]), axis=0)

    tiles(live_ref, body)
    per_block = BLOCK // LANES
    for t in range(peak.shape[0]):
        top = jnp.max(peak[t], axis=0, keepdims=True)
        mass = jnp.sum(total[t] * jnp.exp(peak[t] - top), axis=0, keepdims=True)
        for k, part in enumerate(lane_parts(safe_log(top, mass))):
            packed[t * per_block + k : t * per_block + k + 1, :] = part
    out_ref[...] = jnp.broadcast_to(packed[...][None], out_ref.shape)


def map_kernel(live_ref, rows_ref, tgt_ref, lse_ref, log_ref, c_ref, out_ref, crow, q, peak, denom, numer, buf):
    width = tgt_ref.shape[0]
    c = EPS * log_ref[...] - EPS * logsum(lse_ref[...], 0)[0]
    c_ref[...] = c
    for k in range(c.shape[0]):
        crow[:, k * LANES : (k + 1) * LANES] = c[k : k + 1, :] * INV
    blocks, columns = live_ref.shape
    peak[...] = jnp.full_like(peak, NEG)
    denom[...] = jnp.zeros_like(denom)
    numer[...] = jnp.zeros_like(numer)

    def first(b, t):
        at = pl.ds(pl.multiple_of(t * BLOCK, BLOCK), BLOCK)
        values = score(rows_ref, tgt_ref, b, t) * INV + crow[:, at]
        q[b * columns + t] = values
        peak[b] = functools.reduce(jnp.maximum, lane_parts(values), peak[b])

    tiles(live_ref, first)
    tops = []
    for b in range(blocks):
        tops.append(jnp.max(peak[b].T, axis=0, keepdims=True))
        peak[b] = jnp.broadcast_to(jnp.max(peak[b], axis=1, keepdims=True), peak[b].shape)

    def second(b, t):
        at = pl.ds(pl.multiple_of(t * BLOCK, BLOCK), BLOCK)
        top = jnp.concatenate([peak[b]] * (BLOCK // LANES), axis=1)
        weights = jnp.exp(q[b * columns + t] - top).astype(BF16)
        denom[b] = denom[b] + sum(lane_parts(weights.astype(F32)))
        numer[b] = numer[b] + lax.dot_general(tgt_ref[:, at], weights, NT, preferred_element_type=F32)

    tiles(live_ref, second)
    part = width // GROUPS
    chunk = out_ref.shape[2]
    for b in range(blocks):
        mass = jnp.sum(denom[b].T, axis=0, keepdims=True)
        inverse = 1.0 / jnp.where(mass > 0.0, mass, 1.0)
        logs = three_parts(safe_log(tops[b], mass))
        for k in range(GROUPS):
            buf[:part, :] = numer[b, k * part : (k + 1) * part, :] * inverse
            for j in range(3):
                buf[part + j : part + j + 1, :] = logs[j]
            buf[part + 3 :, :] = jnp.zeros_like(buf[part + 3 :, :])
            for r in range(BLOCK // chunk):
                place = (b * (BLOCK // chunk) + r) * GROUPS + k
                out_ref[place] = buf[:, r * chunk : (r + 1) * chunk].astype(BF16)


def merge_kernel(part, in_ref, out_ref, logs, buf):
    count = in_ref.shape[0]
    for t in range(count):
        tail = in_ref[t].astype(F32)
        logs[t : t + 1, :] = tail[part : part + 1] + tail[part + 1 : part + 2] + tail[part + 2 : part + 3]
    top = jnp.max(logs[...], axis=0, keepdims=True)
    share = jnp.exp(logs[...] - top)
    mass = jnp.sum(share, axis=0, keepdims=True)
    logs[...] = share / mass
    acc = jnp.zeros(in_ref.shape[1:], F32)
    for t in range(count):
        acc = acc + in_ref[t].astype(F32) * logs[t : t + 1, :]
    buf[...] = acc
    for j, piece in enumerate(three_parts(top + jnp.log(mass))):
        buf[part + j : part + j + 1, :] = piece
    out_ref[...] = jnp.broadcast_to(buf[...].astype(BF16)[None], out_ref.shape)


def final_kernel(part, in_ref, f_ref, mapped_ref, mass_ref, buf):
    chunk = in_ref.shape[2]
    per = chunk // LANES
    for r in range(in_ref.shape[0] // GROUPS):
        for k in range(GROUPS):
            piece = in_ref[r * GROUPS + k].astype(F32)
            buf[k * part : (k + 1) * part, :] = piece[:part]
        mapped_ref[:, r * chunk : (r + 1) * chunk] = buf[: GROUPS * part, :].astype(BF16)
        total = piece[part : part + 1] + piece[part + 1 : part + 2] + piece[part + 2 : part + 3]
        for j in range(per):
            at = r * per + j
            own = f_ref[at : at + 1, :] * INV
            mass_ref[at : at + 1, :] = own + total[:, j * LANES : (j + 1) * LANES]


VMEM = pl.BlockSpec(memory_space=pltpu.VMEM)
SMEM = pl.BlockSpec(memory_space=pltpu.SMEM)
PARAMS = pltpu.CompilerParams(vmem_limit_bytes=40 * 1024 * 1024)


def call(kernel, out_shape, scratch, *args, scalars=0):
    specs = [SMEM] * scalars + [VMEM] * (len(args) - scalars)
    return pl.pallas_call(
        kernel,
        out_shape=out_shape,
        in_specs=specs,
        out_specs=jax.tree.map(lambda _: VMEM, out_shape),
        scratch_shapes=scratch,
        compiler_params=PARAMS,
    )(*args)


def local(src_emb, tgt_emb, g_init, log_src, log_tgt, cand_ids, cand_count):
    s_rows, width = src_emb.shape
    t_cols = tgt_emb.shape[0]
    blocks, columns = s_rows // BLOCK, t_cols // BLOCK
    n_tgt, n_src = lax.axis_size("tgt"), lax.axis_size("src")
    shape = jax.ShapeDtypeStruct
    vmem = pltpu.VMEM

    slot = lax.broadcasted_iota(jnp.int32, cand_ids.shape, 1)
    owned = lax.axis_index("tgt") * columns + lax.broadcasted_iota(jnp.int32, (1, 1, columns), 2)
    asked = (cand_ids[:, :, None] == owned) & (slot < cand_count[:, None])[:, :, None]
    live = jnp.max(asked.astype(jnp.int32), axis=1)

    src_t, tgt_t = src_emb.T, tgt_emb.T
    s_tile = (s_rows // LANES, LANES)
    t_tile = (t_cols // LANES, LANES)
    padded = -(-width // LANES) * LANES

    rows, lse = call(
        row_kernel,
        (shape((s_rows, padded), BF16), shape((n_tgt, *s_tile), F32)),
        [
            vmem((padded, s_rows), F32),
            vmem((blocks, BLOCK, LANES), F32),
            vmem((blocks, BLOCK, LANES), F32),
            vmem(s_tile, F32),
        ],
        live, src_t, tgt_t, g_init.reshape(1, t_cols),
        scalars=1,
    )
    lse = lax.all_to_all(lse, "tgt", 0, 0, tiled=True)
    f, lse = call(
        col_kernel,
        (shape(s_tile, F32), shape((n_src, *t_tile), F32)),
        [
            vmem((s_rows, LANES), F32),
            vmem((columns, 8, BLOCK), F32),
            vmem((columns, 8, BLOCK), F32),
            vmem(t_tile, F32),
        ],
        live, rows, tgt_t, lse, log_src.reshape(s_tile),
        scalars=1,
    )
    lse = lax.all_to_all(lse, "src", 0, 0, tiled=True)
    chunk = s_rows * GROUPS // n_tgt
    c, sums = call(
        map_kernel,
        (shape(t_tile, F32), shape((n_tgt, CHUNK, chunk), BF16)),
        [
            vmem((1, t_cols), F32),
            vmem((blocks * columns, BLOCK, BLOCK), F32),
            vmem((blocks, BLOCK, LANES), F32),
            vmem((blocks, BLOCK, LANES), F32),
            vmem((blocks, width, BLOCK), F32),
            vmem((CHUNK, BLOCK), F32),
        ],
        live, rows, tgt_t, lse, log_tgt.reshape(t_tile),
        scalars=1,
    )
    sums = lax.all_to_all(sums, "tgt", 0, 0, tiled=True)
    part = width // GROUPS
    sums = call(
        functools.partial(merge_kernel, part),
        shape((n_tgt, CHUNK, chunk), BF16),
        [vmem((n_tgt, chunk), F32), vmem((CHUNK, chunk), F32)],
        sums,
    )
    sums = lax.all_to_all(sums, "tgt", 0, 0, tiled=True)
    mapped, mass = call(
        functools.partial(final_kernel, part),
        (shape((width, s_rows), BF16), shape(s_tile, F32)),
        [vmem((-(-width // 8) * 8, chunk), F32)],
        sums, f,
    )
    return f.reshape(s_rows), c.reshape(t_cols), mapped.T, mass.reshape(s_rows)


def solution(mesh):
    return jax.shard_map(
        local,
        mesh=mesh,
        in_specs=(
            P("src", None),
            P("tgt", None),
            P("tgt"),
            P("src"),
            P("tgt"),
            P("src", None),
            P("src"),
        ),
        out_specs=(P("src"), P("tgt"), P("src", None), P("src")),
        check_vma=False,
    )
```

time: 447 us -> 121 us (0.27)
  the two profiles are of different devices: /device:TPU:1 before, /device:TPU:16 now
where the time goes in v1:
time: 121 us
  blocking collectives  89.8 us (74%)
  Pallas kernels  25.3 us (21%)
  local copies, waits for them, and re-layouts  3.51 us (3%)
  other arithmetic  1.59 us (1%)
    all_to_all x2, blocking collectives, local(): sums = lax.all_to_all(sums, 'tgt', 0, 0, tiled=True)  50 us
    pallas_call x5, Pallas kernels, call(): pl.pallas_call(kernel, out_shape=out_shape, in_specs=specs, out_specs=jax...  25.3 us
    all_to_all x1, blocking collectives, local(): lse = lax.all_to_all(lse, 'tgt', 0, 0, tiled=True)  22.7 us
    all_to_all x1, blocking collectives, local(): lse = lax.all_to_all(lse, 'src', 0, 0, tiled=True)  17.1 us
    unnamed x14, local copies, waits for them, and re-layouts  3.51 us

profile of v1, /device:TPU:16, one launch (start us, length us, event | category | flops | bytes accessed | tf_op | source)
XLA Modules:
  0.0 120.8 jit_solution(15645299974273395271)
XLA Ops:
  0.6 0.0 copy-start.5
  0.7 0.7 iota_compare_fusion
  1.4 0.9 convert_reduce_fusion.live_ref
  2.2 0.0 copy-start
  2.3 1.7 %copy-done = bf16[4096,300]{0,1:T(8,128)(2,1)S(1)} copy-done((bf16[4096,300]{0,1:T(8,128)(2,1)S(1)}, bf16[4096,300]{0,1:T(8,128)(2,1)}, u32[]{:S(2)}) %copy-start) | copy-done | bytes 2457624
  4.0 0.0 copy-start.2
  4.0 1.1 copy-done.2
  5.0 0.0 copy-start.3
  5.0 0.7 copy-done.3
  5.7 0.0 copy-start.1
  5.7 6.7 %shard_map.102 = (bf16[1024,384]{1,0:T(8,128)(2,1)S(1)}, f32[32,8,128]{2,1,0:T(8,128)S(1)}) custom-call(s32[2,8]{1,0:T(2,128)S(1)} %convert_reduce_fusion.live_ref, bf16[300,1024]{1,0:T(8,128)(2,1)S(1)} %bitcast.12, bf16[300,4096]{1,0:T(8,128)(2,1)S(1)} %bitcast.9, f32[1,4096]{1,0:T(1,128)S(1)} %bitcast.13), custom_call_target="tpu_custom_call" | custom-call | tf_op jit(solution)/shard_map/pallas_call | solution.py:207
  12.5 0.0 copy-start.4
  12.5 22.7 %all_to_all.20.lse_ref = f32[32,8,128]{2,1,0:T(8,128)S(1)} all-to-all(f32[32,8,128]{2,1,0:T(8,128)S(1)} %get-tuple-element.13), channel_id=1, replica_groups=mesh['tgt'=32,'src'=16] {'tgt'}, dimensions={0} | all-to-all | bytes 262144 | tf_op jit(solution)/shard_map/all_to_all | solution.py:247
  35.2 0.0 copy-done.5
  35.2 0.0 copy-done.1
  35.2 7.1 %shard_map.103 = (f32[8,128]{1,0:T(8,128)}, f32[16,32,128]{2,1,0:T(8,128)S(1)}) custom-call(s32[2,8]{1,0:T(2,128)S(1)} %convert_reduce_fusion.live_ref, bf16[1024,384]{1,0:T(8,128)(2,1)S(1)} %get-tuple-element.12.rows_ref, bf16[300,4096]{1,0:T(8,128)(2,1)S(1)} %bitcast.10, f32[32,8,128]{2,1,0:T(8,128)S(1)} %all_to_all.20.lse_ref, f32[8,128]{1,0:T(8,128)S(1)} %bitcast.15), custom_call_target="tpu_custom_call" | custom-call | tf_op jit(solution)/shard_map/pallas_call | solution.py:207
  42.3 17.1 %all_to_all.21.lse_ref = f32[16,32,128]{2,1,0:T(8,128)S(1)} all-to-all(f32[16,32,128]{2,1,0:T(8,128)S(1)} %get-tuple-element.15), channel_id=1, replica_groups=mesh['tgt'=32,'src'=16] {'src'}, dimensions={0} | all-to-all | bytes 524288 | tf_op jit(solution)/shard_map/all_to_all | solution.py:260
  59.4 0.0 copy-done.4
  59.4 10.1 %shard_map.104 = (f32[32,128]{1,0:T(8,128)}, bf16[32,80,128]{2,1,0:T(8,128)(2,1)S(1)}) custom-call(s32[2,8]{1,0:T(2,128)S(1)} %convert_reduce_fusion.live_ref, bf16[1024,384]{1,0:T(8,128)(2,1)S(1)} %get-tuple-element.12.rows_ref, bf16[300,4096]{1,0:T(8,128)(2,1)S(1)} %bitcast.11, f32[16,32,128]{2,1,0:T(8,128)S(1)} %all_to_all.21.lse_ref, f32[32,128]{1,0:T(8,128)S(1)} %bitcast.14), custom_call_target="tpu_custom_call" | custom-call | tf_op jit(solution)/shard_map/pallas_call | solution.py:207
  69.6 24.1 %all_to_all.22.in_ref = bf16[32,80,128]{2,1,0:T(8,128)(2,1)S(1)} all-to-all(bf16[32,80,128]{2,1,0:T(8,128)(2,1)S(1)} %get-tuple-element.17), channel_id=1, replica_groups=mesh['tgt'=32,'src'=16] {'tgt'}, dimensions={0} | all-to-all | bytes 1310720 | tf_op jit(solution)/shard_map/all_to_all | solution.py:276
  93.7 0.2 shard_map.105
  93.9 25.8 %all_to_all.23.in_ref = bf16[32,80,128]{2,1,0:T(8,128)(2,1)S(1)} all-to-all(bf16[32,80,128]{2,1,0:T(8,128)(2,1)S(1)} %shard_map.105), channel_id=1, replica_groups=mesh['tgt'=32,'src'=16] {'tgt'}, dimensions={0} | all-to-all | bytes 1310720 | tf_op jit(solution)/shard_map/all_to_all | solution.py:284
  119.8 0.0 copy-done.6
  119.8 1.1 shard_map.106
  (2 shorter events, 0.0 us)
Async XLA Ops:
  0.6 34.5 %copy-start.5 = (f32[1024]{0:T(1024)S(1)}, f32[1024]{0:T(1024)}, u32[]{:S(2)}) copy-start(f32[1024]{0:T(1024)} %param.10) | copy-start | bytes 12292
  2.2 1.7 %copy-start = (bf16[4096,300]{0,1:T(8,128)(2,1)S(1)}, bf16[4096,300]{0,1:T(8,128)(2,1)}, u32[]{:S(2)}) copy-start(bf16[4096,300]{0,1:T(8,128)(2,1)} %param.8) | copy-start | bytes 7372804
  4.0 1.1 copy-start.2
  5.0 0.7 copy-start.3
  5.7 29.4 %copy-start.1 = (bf16[4096,300]{0,1:T(8,128)(2,1)S(1)}, bf16[4096,300]{0,1:T(8,128)(2,1)}, u32[]{:S(2)}) copy-start(bf16[4096,300]{0,1:T(8,128)(2,1)} %param.8) | copy-start | bytes 7372804
  12.5 47.0 %copy-start.4 = (f32[4096]{0:T(1024)S(1)}, f32[4096]{0:T(1024)}, u32[]{:S(2)}) copy-start(f32[4096]{0:T(1024)} %param.11) | copy-start | bytes 49156
  69.6 50.2 %copy-start.6 = (f32[8,128]{1,0:T(8,128)S(1)}, f32[8,128]{1,0:T(8,128)}, u32[]{:S(2)}) copy-start(f32[8,128]{1,0:T(8,128)} %get-tuple-element.14.f_ref) | copy-start | bytes 12292

commit v2 on v1

v2 whole, which is shorter than its diff:
```python
import functools
import itertools

import jax
import jax.numpy as jnp
from jax import lax
from jax.experimental import pallas as pl
from jax.experimental.pallas import tpu as pltpu
from jax.sharding import PartitionSpec as P

BLOCK = 512
LANES = 128
EPS = 0.2
INV = 5.0
LN2 = 0.6931471805599453
SCALE = INV / LN2
STRIP = 32
NEG = -1e30
GROUPS = 4
CHUNK = 80
NT = (((1,), (1,)), ((), ()))
F32 = jnp.float32
BF16 = jnp.bfloat16


def logsum(values, axis):
    peak = jnp.max(values, axis=axis, keepdims=True)
    return peak + jnp.log(jnp.sum(jnp.exp(values - peak), axis=axis, keepdims=True))


def safe_log(peak, total):
    return jnp.where(total > 0.0, peak * LN2 + jnp.log(jnp.where(total > 0.0, total, 1.0)), NEG)


def lane_parts(tile):
    return [tile[:, k * LANES : (k + 1) * LANES] for k in range(tile.shape[1] // LANES)]


def three_parts(value):
    high = value.astype(BF16).astype(F32)
    rest = value - high
    middle = rest.astype(BF16).astype(F32)
    return high, middle, rest - middle


def pick(order_ref, i, columns):
    last = order_ref.shape[0] - 1
    place = order_ref[jnp.minimum(i, last - 1)]
    return place, place // columns, place % columns, i < order_ref[last]


def in_turn(order_ref, columns, make, use):
    tile = functools.partial(pick, order_ref, columns=columns)
    make(0, tile(0))

    def step(k, carry):
        i = 2 * k
        make(1, tile(i + 1))
        use(0, tile(i))
        make(0, tile(i + 2))
        use(1, tile(i + 1))
        return carry

    lax.fori_loop(0, (order_ref[order_ref.shape[0] - 1] + 1) // 2, step, 0)


def each(order_ref, columns, use):
    tile = functools.partial(pick, order_ref, columns=columns)

    def step(k, carry):
        use(tile(2 * k))
        use(tile(2 * k + 1))
        return carry

    lax.fori_loop(0, (order_ref[order_ref.shape[0] - 1] + 1) // 2, step, 0)


def block_of(index):
    return pl.ds(pl.multiple_of(index * BLOCK, BLOCK), BLOCK)


def row_kernel(
    first_ref, count_hbm, ids_hbm, src_hbm, tgt_hbm, g_hbm, log_src_hbm, log_tgt_hbm,
    scores_ref, out_ref, order_ref, log_src_ref, log_tgt_ref,
    count_ref, ids_ref, src_ref, tgt_ref, g_ref, pad, rows_ref, peak, total, packed, slot0, slot1, sems,
):
    pairs = (
        (count_hbm, count_ref), (ids_hbm, ids_ref), (src_hbm, src_ref), (tgt_hbm, tgt_ref),
        (g_hbm, g_ref), (log_src_hbm, log_src_ref), (log_tgt_hbm, log_tgt_ref),
    )
    copies = [pltpu.make_async_copy(x, y, sems.at[i]) for i, (x, y) in enumerate(pairs)]
    for copy in copies:
        copy.start()
    width, s_rows = src_ref.shape
    blocks, columns = s_rows // BLOCK, tgt_ref.shape[1] // BLOCK
    peak[...] = jnp.full_like(peak, NEG)
    total[...] = jnp.zeros_like(total)

    copies[0].wait()
    copies[1].wait()
    lane = lax.broadcasted_iota(jnp.int32, (1, ids_ref.shape[1]), 1)
    live = []
    for b in range(blocks):
        rel = jnp.where(lane < count_ref[b], ids_ref[b : b + 1, :] - first_ref[0], -1)
        for t in range(columns):
            live.append(jnp.max(jnp.where(rel == t, 1.0, 0.0)) > 0.0)
    count = jnp.int32(0)
    latest = jnp.int32(0)
    for place, there in enumerate(live):
        latest = jnp.where(there, place, latest)
        order_ref[count] = latest
        count = count + there.astype(jnp.int32)

    def fill(i, carry):
        order_ref[i] = latest
        return carry

    lax.fori_loop(count, blocks * columns, fill, 0)
    order_ref[blocks * columns] = count

    copies[2].wait()
    edge = width // 8 * 8
    pad[edge:, :] = jnp.zeros_like(pad[edge:, :])
    pad[:width, :] = src_ref[...].astype(F32)
    for k in range(s_rows // LANES):
        piece = pad[:, k * LANES : (k + 1) * LANES]
        rows_ref[k * LANES : (k + 1) * LANES, :] = piece.T.astype(BF16)
    for copy in copies[3:]:
        copy.wait()

    slots = (slot0, slot1)

    def make(n, tile):
        place, b, t, there = tile
        rows = rows_ref[block_of(b), :]
        slots[n][...] = jnp.dot(rows[:, :width], tgt_ref[:, block_of(t)], preferred_element_type=F32)

    def use(n, tile):
        place, b, t, there = tile
        g = jnp.where(there, g_ref[:, block_of(t)] * SCALE, 2 * NEG)
        for r in range(0, BLOCK, STRIP):
            at = slice(r, r + STRIP)
            values = slots[n][at, :]
            scores_ref[place, at, :] = values
            z = lane_parts(values * SCALE + g)
            old = peak[b, at, :]
            new = functools.reduce(jnp.maximum, z, old)
            peak[b, at, :] = new
            total[b, at, :] = total[b, at, :] * jnp.exp2(old - new) + sum(jnp.exp2(part - new) for part in z)

    in_turn(order_ref, columns, make, use)
    per_block = BLOCK // LANES
    for b in range(blocks):
        turned = peak[b].T
        top = jnp.max(turned, axis=0, keepdims=True)
        mass = jnp.sum(total[b].T * jnp.exp2(turned - top), axis=0, keepdims=True)
        for k, part in enumerate(lane_parts(safe_log(top, mass))):
            packed[b * per_block + k : b * per_block + k + 1, :] = part
    out_ref[...] = jnp.broadcast_to(packed[...][None], out_ref.shape)


def col_kernel(order_ref, scores_ref, lse_ref, log_ref, f_ref, out_ref, fcol, peak, total, packed, slot0, slot1):
    f = EPS * log_ref[...] - EPS * logsum(lse_ref[...], 0)[0]
    f_ref[...] = f
    for k in range(f.shape[0]):
        row = jnp.broadcast_to(f[k : k + 1, :] * SCALE, (LANES, LANES))
        fcol[k * LANES : (k + 1) * LANES, :] = row.T
    peak[...] = jnp.full_like(peak, NEG)
    total[...] = jnp.zeros_like(total)
    columns = peak.shape[0]

    def use(slot, tile):
        place, b, t, there = tile
        extra = jnp.where(there, 0.0, 2 * NEG)
        old = peak[t]
        tops = [old] * 2
        for n, r in enumerate(range(0, BLOCK, STRIP)):
            at = slice(r, r + STRIP)
            own = fcol[pl.ds(pl.multiple_of(b * BLOCK + r, STRIP), STRIP), :] + extra
            y = scores_ref[place, at, :] * SCALE + jnp.concatenate([own] * (BLOCK // LANES), axis=1)
            slot[at, :] = y
            tops[n % 2] = jnp.maximum(tops[n % 2], jnp.max(y.reshape(STRIP // 8, 8, BLOCK), axis=0))
        new = jnp.maximum(*tops)
        peak[t] = new
        sums = [total[t] * jnp.exp2(old - new), jnp.zeros_like(new)]
        for n, r in enumerate(range(0, BLOCK, STRIP)):
            y = slot[slice(r, r + STRIP), :].reshape(STRIP // 8, 8, BLOCK)
            sums[n % 2] = sums[n % 2] + jnp.sum(jnp.exp2(y - new[None]), axis=0)
        total[t] = sums[0] + sums[1]

    slots = itertools.cycle((slot0, slot1))
    each(order_ref, columns, lambda tile: use(next(slots), tile))
    per_block = BLOCK // LANES
    for t in range(columns):
        top = jnp.max(peak[t], axis=0, keepdims=True)
        mass = jnp.sum(total[t] * jnp.exp2(peak[t] - top), axis=0, keepdims=True)
        for k, part in enumerate(lane_parts(safe_log(top, mass))):
            packed[t * per_block + k : t * per_block + k + 1, :] = part
    out_ref[...] = jnp.broadcast_to(packed[...][None], out_ref.shape)


def map_kernel(
    order_ref, scores_ref, tgt_ref, lse_ref, log_ref, c_ref, out_ref,
    crow, peak, denom, numer, buf, part0, part1,
):
    width = tgt_ref.shape[0]
    c = EPS * log_ref[...] - EPS * logsum(lse_ref[...], 0)[0]
    c_ref[...] = c
    for k in range(c.shape[0]):
        crow[:, k * LANES : (k + 1) * LANES] = c[k : k + 1, :] * SCALE
    blocks, columns = peak.shape[0], tgt_ref.shape[1] // BLOCK
    peak[...] = jnp.full_like(peak, NEG)
    denom[...] = jnp.zeros_like(denom)
    numer[...] = jnp.zeros_like(numer)

    def first(tile):
        place, b, t, there = tile
        own = crow[:, block_of(t)]
        for r in range(0, BLOCK, STRIP):
            at = slice(r, r + STRIP)
            values = scores_ref[place, at, :] * SCALE + own
            peak[b, at, :] = functools.reduce(jnp.maximum, lane_parts(values), peak[b, at, :])

    each(order_ref, columns, first)
    tops = []
    for b in range(blocks):
        tops.append(jnp.max(peak[b].T, axis=0, keepdims=True))
        peak[b] = jnp.broadcast_to(jnp.max(peak[b], axis=1, keepdims=True), peak[b].shape)

    slots = (part0, part1)

    def weigh(n, tile):
        place, b, t, there = tile
        extra = jnp.where(there, 0.0, -NEG)
        own = crow[:, block_of(t)]
        for r in range(0, BLOCK, STRIP):
            at = slice(r, r + STRIP)
            top = peak[b, at, :] + extra
            values = scores_ref[place, at, :] * SCALE + own
            weights = [jnp.exp2(part - top).astype(BF16) for part in lane_parts(values)]
            slots[n][at, :] = jnp.concatenate(weights, axis=1)
            denom[b, at, :] = denom[b, at, :] + sum(part.astype(F32) for part in weights)

    def add(n, tile):
        place, b, t, there = tile
        numer[b] = numer[b] + lax.dot_general(tgt_ref[:, block_of(t)], slots[n][...], NT, preferred_element_type=F32)

    @pl.when(order_ref[order_ref.shape[0] - 1] > 0)
    def _():
        in_turn(order_ref, columns, weigh, add)

    part = width // GROUPS
    chunk = out_ref.shape[2]
    for b in range(blocks):
        mass = jnp.sum(denom[b].T, axis=0, keepdims=True)
        inverse = 1.0 / jnp.where(mass > 0.0, mass, 1.0)
        logs = three_parts(safe_log(tops[b], mass))
        for k in range(GROUPS):
            buf[:part, :] = numer[b, k * part : (k + 1) * part, :] * inverse
            for j in range(3):
                buf[part + j : part + j + 1, :] = logs[j]
            buf[part + 3 :, :] = jnp.zeros_like(buf[part + 3 :, :])
            for r in range(BLOCK // chunk):
                place = (b * (BLOCK // chunk) + r) * GROUPS + k
                out_ref[place] = buf[:, r * chunk : (r + 1) * chunk].astype(BF16)


def merge_kernel(part, in_ref, out_ref, logs, buf):
    count = in_ref.shape[0]
    for t in range(count):
        tail = in_ref[t].astype(F32)
        logs[t : t + 1, :] = tail[part : part + 1] + tail[part + 1 : part + 2] + tail[part + 2 : part + 3]
    top = jnp.max(logs[...], axis=0, keepdims=True)
    share = jnp.exp(logs[...] - top)
    mass = jnp.sum(share, axis=0, keepdims=True)
    logs[...] = share / mass
    acc = jnp.zeros(in_ref.shape[1:], F32)
    for t in range(count):
        acc = acc + in_ref[t].astype(F32) * logs[t : t + 1, :]
    buf[...] = acc
    for j, piece in enumerate(three_parts(top + jnp.log(mass))):
        buf[part + j : part + j + 1, :] = piece
    out_ref[...] = jnp.broadcast_to(buf[...].astype(BF16)[None], out_ref.shape)


def final_kernel(part, in_ref, f_ref, mapped_ref, mass_ref, buf):
    chunk = in_ref.shape[2]
    per = chunk // LANES
    for r in range(in_ref.shape[0] // GROUPS):
        for k in range(GROUPS):
            piece = in_ref[r * GROUPS + k].astype(F32)
            buf[k * part : (k + 1) * part, :] = piece[:part]
        mapped_ref[:, r * chunk : (r + 1) * chunk] = buf[: GROUPS * part, :].astype(BF16)
        total = piece[part : part + 1] + piece[part + 1 : part + 2] + piece[part + 2 : part + 3]
        for j in range(per):
            at = r * per + j
            own = f_ref[at : at + 1, :] * INV
            mass_ref[at : at + 1, :] = own + total[:, j * LANES : (j + 1) * LANES]


VMEM = pl.BlockSpec(memory_space=pltpu.VMEM)
SMEM = pl.BlockSpec(memory_space=pltpu.SMEM)
HBM = pl.BlockSpec(memory_space=pltpu.HBM)
PARAMS = pltpu.CompilerParams(vmem_limit_bytes=24 * 1024 * 1024)


def call(kernel, out_shape, scratch, specs, *args, outs=None):
    return pl.pallas_call(
        kernel,
        out_shape=out_shape,
        in_specs=specs,
        out_specs=jax.tree.map(lambda _: VMEM, out_shape) if outs is None else outs,
        scratch_shapes=scratch,
        compiler_params=PARAMS,
    )(*args)


def run_rows(first, count, ids, src_t, tgt_t, g, log_src, log_tgt, n_tgt):
    (width, s_rows), t_cols = src_t.shape, tgt_t.shape[1]
    blocks, columns = s_rows // BLOCK, t_cols // BLOCK
    padded = -(-width // LANES) * LANES
    s_tile = (s_rows // LANES, LANES)
    return call(
        row_kernel,
        (
            jax.ShapeDtypeStruct((blocks * columns, BLOCK, BLOCK), F32),
            jax.ShapeDtypeStruct((n_tgt, *s_tile), F32),
            jax.ShapeDtypeStruct((blocks * columns + 1,), jnp.int32),
            jax.ShapeDtypeStruct(log_src.shape, F32),
            jax.ShapeDtypeStruct(log_tgt.shape, F32),
        ),
        [
            pltpu.SMEM(count.shape, jnp.int32),
            pltpu.VMEM(ids.shape, jnp.int32),
            pltpu.VMEM(src_t.shape, BF16),
            pltpu.VMEM(tgt_t.shape, BF16),
            pltpu.VMEM(g.shape, F32),
            pltpu.VMEM((padded, s_rows), F32),
            pltpu.VMEM((s_rows, padded), BF16),
            pltpu.VMEM((blocks, BLOCK, LANES), F32),
            pltpu.VMEM((blocks, BLOCK, LANES), F32),
            pltpu.VMEM(s_tile, F32),
            pltpu.VMEM((BLOCK, BLOCK), F32),
            pltpu.VMEM((BLOCK, BLOCK), F32),
            pltpu.SemaphoreType.DMA((7,)),
        ],
        [SMEM] + [HBM] * 7,
        first, *(pltpu.with_memory_space_constraint(x, pltpu.HBM) for x in (count, ids, src_t, tgt_t, g, log_src, log_tgt)),
        outs=(VMEM, VMEM, SMEM, VMEM, VMEM),
    )


def run_cols(order, scores, lse, log_src, n_src, t_cols):
    s_tile, s_rows = log_src.shape, log_src.size
    t_tile, columns = (t_cols // LANES, LANES), t_cols // BLOCK
    return call(
        col_kernel,
        (jax.ShapeDtypeStruct(s_tile, F32), jax.ShapeDtypeStruct((n_src, *t_tile), F32)),
        [
            pltpu.VMEM((s_rows, LANES), F32),
            pltpu.VMEM((columns, 8, BLOCK), F32),
            pltpu.VMEM((columns, 8, BLOCK), F32),
            pltpu.VMEM(t_tile, F32),
            pltpu.VMEM((BLOCK, BLOCK), F32),
            pltpu.VMEM((BLOCK, BLOCK), F32),
        ],
        [SMEM, VMEM, VMEM, VMEM],
        order, scores, lse, log_src,
    )


def run_map(order, scores, tgt_t, lse, log_tgt, n_tgt, s_rows):
    t_tile, (width, t_cols) = log_tgt.shape, tgt_t.shape
    blocks, columns = s_rows // BLOCK, t_cols // BLOCK
    chunk = s_rows * GROUPS // n_tgt
    return call(
        map_kernel,
        (jax.ShapeDtypeStruct(t_tile, F32), jax.ShapeDtypeStruct((n_tgt, CHUNK, chunk), BF16)),
        [
            pltpu.VMEM((1, t_cols), F32),
            pltpu.VMEM((blocks, BLOCK, LANES), F32),
            pltpu.VMEM((blocks, BLOCK, LANES), F32),
            pltpu.VMEM((blocks, width, BLOCK), F32),
            pltpu.VMEM((CHUNK, BLOCK), F32),
            pltpu.VMEM((BLOCK, BLOCK), BF16),
            pltpu.VMEM((BLOCK, BLOCK), BF16),
        ],
        [SMEM, VMEM, VMEM, VMEM, VMEM],
        order, scores, tgt_t, lse, log_tgt,
    )


def local(src_emb, tgt_emb, g_init, log_src, log_tgt, cand_ids, cand_count):
    s_rows, width = src_emb.shape
    t_cols = tgt_emb.shape[0]
    n_tgt, n_src = lax.axis_size("tgt"), lax.axis_size("src")
    src_t, tgt_t = src_emb.T, tgt_emb.T
    s_tile = (s_rows // LANES, LANES)
    t_tile = (t_cols // LANES, LANES)
    first = (lax.axis_index("tgt") * (t_cols // BLOCK)).astype(jnp.int32).reshape(1)

    scores, lse, order, log_src, log_tgt = run_rows(
        first, cand_count, cand_ids, src_t, tgt_t, g_init.reshape(1, t_cols),
        log_src.reshape(s_tile), log_tgt.reshape(t_tile), n_tgt,
    )
    lse = lax.all_to_all(lse, "tgt", 0, 0, tiled=True)
    f, lse = run_cols(order, scores, lse, log_src, n_src, t_cols)
    lse = lax.all_to_all(lse, "src", 0, 0, tiled=True)
    c, sums = run_map(order, scores, tgt_t, lse, log_tgt, n_tgt, s_rows)
    sums = lax.all_to_all(sums, "tgt", 0, 0, tiled=True)
    part, chunk = width // GROUPS, sums.shape[2]
    sums = call(
        functools.partial(merge_kernel, part),
        jax.ShapeDtypeStruct(sums.shape, BF16),
        [pltpu.VMEM((n_tgt, chunk), F32), pltpu.VMEM((CHUNK, chunk), F32)],
        [VMEM],
        sums,
    )
    sums = lax.all_to_all(sums, "tgt", 0, 0, tiled=True)
    mapped, mass = call(
        functools.partial(final_kernel, part),
        (jax.ShapeDtypeStruct((width, s_rows), BF16), jax.ShapeDtypeStruct(s_tile, F32)),
        [pltpu.VMEM((-(-width // 8) * 8, chunk), F32)],
        [VMEM, VMEM],
        sums, f,
    )
    return f.reshape(s_rows), c.reshape(t_cols), mapped.T, mass.reshape(s_rows)


def solution(mesh):
    return jax.shard_map(
        local,
        mesh=mesh,
        in_specs=(
            P("src", None),
            P("tgt", None),
            P("tgt"),
            P("src"),
            P("tgt"),
            P("src", None),
            P("src"),
        ),
        out_specs=(P("src"), P("tgt"), P("src", None), P("src")),
        check_vma=False,
    )
```

time: 121 us -> 111 us (0.917)
  the two profiles are of different devices: /device:TPU:16 before, /device:TPU:1 now
where the time goes in v2:
time: 111 us; the launch traced here: 110 us
  blocking collectives  96.8 us (87%)
  Pallas kernels  12.8 us (12%)
    all_to_all x2, blocking collectives, local(): sums = lax.all_to_all(sums, 'tgt', 0, 0, tiled=True)  49.3 us
    all_to_all x1, blocking collectives, local(): lse = lax.all_to_all(lse, 'tgt', 0, 0, tiled=True)  26.6 us
    all_to_all x1, blocking collectives, local(): lse = lax.all_to_all(lse, 'src', 0, 0, tiled=True)  20.9 us
    pallas_call x5, Pallas kernels, call(): pl.pallas_call(kernel, out_shape=out_shape, in_specs=specs, out_specs=jax...  12.8 us

profile of v2, /device:TPU:1, one launch (start us, length us, event | category | flops | bytes accessed | tf_op | source)
XLA Modules:
  0.0 110.3 jit_solution(18340888654278276261)
XLA Ops:
  0.6 0.0 copy-start
  0.6 5.0 %shard_map.102 = (f32[16,512,512]{2,1,0:T(8,128)S(1)}, f32[32,8,128]{2,1,0:T(8,128)S(1)}, s32[17]{0:T(128)S(1)}, f32[8,128]{1,0:T(8,128)S(1)}, f32[32,128]{1,0:T(8,128)S(1)}) custom-call(s32[1]{0:T(128)} %bitcast.first_ref, s32[2]{0:T(128)} %count_hbm.1, s32[2,128]{1,0:T(2,128)} %ids_hbm.1, bf16[300,1024]{1,0:T(8,128)(2,1)} %bitcast.13, ...), custom_call_target="tpu_custom_call" | custom-call | tf_op jit(solution)/shard_map/pallas_call | solution.py:308
  5.6 26.6 %all_to_all.20.lse_ref = f32[32,8,128]{2,1,0:T(8,128)S(1)} all-to-all(f32[32,8,128]{2,1,0:T(8,128)S(1)} %get-tuple-element.17), channel_id=1, replica_groups=mesh['tgt'=32,'src'=16] {'tgt'}, dimensions={0} | all-to-all | bytes 262144 | tf_op jit(solution)/shard_map/all_to_all | solution.py:406
  32.2 2.5 %shard_map.103 = (f32[8,128]{1,0:T(8,128)}, f32[16,32,128]{2,1,0:T(8,128)S(1)}) custom-call(s32[17]{0:T(128)S(1)} %get-tuple-element.15.order_ref, f32[16,512,512]{2,1,0:T(8,128)S(1)} %get-tuple-element.16.scores_ref, f32[32,8,128]{2,1,0:T(8,128)S(1)} %all_to_all.20.lse_ref, f32[8,128]{1,0:T(8,128)S(1)} %get-tuple-element.18.log_ref), custom_call_target="tpu_custom_call" | custom-call | tf_op jit(solution)/shard_map/pallas_call | solution.py:308
  34.7 0.0 copy-start.1
  34.7 20.9 %all_to_all.21.lse_ref = f32[16,32,128]{2,1,0:T(8,128)S(1)} all-to-all(f32[16,32,128]{2,1,0:T(8,128)S(1)} %get-tuple-element.20), channel_id=1, replica_groups=mesh['tgt'=32,'src'=16] {'src'}, dimensions={0} | all-to-all | bytes 524288 | tf_op jit(solution)/shard_map/all_to_all | solution.py:408
  55.6 0.0 copy-done
  55.6 4.1 %shard_map.104 = (f32[32,128]{1,0:T(8,128)}, bf16[32,80,128]{2,1,0:T(8,128)(2,1)S(1)}) custom-call(s32[17]{0:T(128)S(1)} %get-tuple-element.15.order_ref, f32[16,512,512]{2,1,0:T(8,128)S(1)} %get-tuple-element.16.scores_ref, bf16[300,4096]{1,0:T(8,128)(2,1)S(1)} %bitcast.11, f32[16,32,128]{2,1,0:T(8,128)S(1)} %all_to_all.21.lse_ref, ...), custom_call_target="tpu_custom_call" | custom-call | tf_op jit(solution)/shard_map/pallas_call | solution.py:308
  59.7 24.7 %all_to_all.22.in_ref = bf16[32,80,128]{2,1,0:T(8,128)(2,1)S(1)} all-to-all(bf16[32,80,128]{2,1,0:T(8,128)(2,1)S(1)} %get-tuple-element.23), channel_id=1, replica_groups=mesh['tgt'=32,'src'=16] {'tgt'}, dimensions={0} | all-to-all | bytes 1310720 | tf_op jit(solution)/shard_map/all_to_all | solution.py:410
  84.4 0.2 shard_map.105
  84.6 24.6 %all_to_all.23.in_ref = bf16[32,80,128]{2,1,0:T(8,128)(2,1)S(1)} all-to-all(bf16[32,80,128]{2,1,0:T(8,128)(2,1)S(1)} %shard_map.105), channel_id=1, replica_groups=mesh['tgt'=32,'src'=16] {'tgt'}, dimensions={0} | all-to-all | bytes 1310720 | tf_op jit(solution)/shard_map/all_to_all | solution.py:419
  109.2 0.0 copy-done.1
  109.2 1.1 shard_map.106
Async XLA Ops:
  0.6 55.0 %copy-start = (bf16[4096,300]{0,1:T(8,128)(2,1)S(1)}, bf16[4096,300]{0,1:T(8,128)(2,1)}, u32[]{:S(2)}) copy-start(bf16[4096,300]{0,1:T(8,128)(2,1)} %param.8) | copy-start | bytes 7372804
  34.7 74.5 %copy-start.1 = (f32[8,128]{1,0:T(8,128)S(1)}, f32[8,128]{1,0:T(8,128)}, u32[]{:S(2)}) copy-start(f32[8,128]{1,0:T(8,128)} %get-tuple-element.19.f_ref) | copy-start | bytes 12292

commit v3 on v2

--- a/solution.py
+++ b/solution.py
@@ -15,6 +15,7 @@
 LN2 = 0.6931471805599453
 SCALE = INV / LN2
 STRIP = 32
+COUNT = 127
 NEG = -1e30
 GROUPS = 4
 CHUNK = 80
@@ -44,9 +45,8 @@
 
 
 def pick(order_ref, i, columns):
-    last = order_ref.shape[0] - 1
-    place = order_ref[jnp.minimum(i, last - 1)]
-    return place, place // columns, place % columns, i < order_ref[last]
+    place = order_ref[0, jnp.minimum(i, COUNT - 1)]
+    return place, place // columns, place % columns, i < order_ref[0, COUNT]
 
 
 def in_turn(order_ref, columns, make, use):
@@ -61,7 +61,7 @@
         use(1, tile(i + 1))
         return carry
 
-    lax.fori_loop(0, (order_ref[order_ref.shape[0] - 1] + 1) // 2, step, 0)
+    lax.fori_loop(0, (order_ref[0, COUNT] + 1) // 2, step, 0)
 
 
 def each(order_ref, columns, use):
@@ -72,7 +72,11 @@
         use(tile(2 * k + 1))
         return carry
 
-    lax.fori_loop(0, (order_ref[order_ref.shape[0] - 1] + 1) // 2, step, 0)
+    lax.fori_loop(0, (order_ref[0, COUNT] + 1) // 2, step, 0)
+
+
+def my_place():
+    return lax.axis_index("tgt").astype(jnp.int32)
 
 
 def block_of(index):
@@ -80,9 +84,9 @@
 
 
 def row_kernel(
-    first_ref, count_hbm, ids_hbm, src_hbm, tgt_hbm, g_hbm, log_src_hbm, log_tgt_hbm,
-    scores_ref, out_ref, order_ref, log_src_ref, log_tgt_ref,
-    count_ref, ids_ref, src_ref, tgt_ref, g_ref, pad, rows_ref, peak, total, packed, slot0, slot1, sems,
+    count_hbm, ids_hbm, src_hbm, tgt_hbm, g_hbm, log_src_hbm, log_tgt_hbm,
+    scores_ref, out_ref, list_ref, log_src_ref, log_tgt_ref,
+    order_ref, count_ref, ids_ref, src_ref, tgt_ref, g_ref, pad, rows_ref, peak, total, packed, slot0, slot1, sems,
 ):
     pairs = (
         (count_hbm, count_ref), (ids_hbm, ids_ref), (src_hbm, src_ref), (tgt_hbm, tgt_ref),
@@ -98,25 +102,29 @@
 
     copies[0].wait()
     copies[1].wait()
+    first = my_place() * columns
     lane = lax.broadcasted_iota(jnp.int32, (1, ids_ref.shape[1]), 1)
     live = []
     for b in range(blocks):
-        rel = jnp.where(lane < count_ref[b], ids_ref[b : b + 1, :] - first_ref[0], -1)
+        rel = jnp.where(lane < count_ref[b], ids_ref[b : b + 1, :] - first, -1)
         for t in range(columns):
             live.append(jnp.max(jnp.where(rel == t, 1.0, 0.0)) > 0.0)
-    count = jnp.int32(0)
     latest = jnp.int32(0)
     for place, there in enumerate(live):
         latest = jnp.where(there, place, latest)
-        order_ref[count] = latest
+    for i in range(len(live)):
+        order_ref[0, i] = latest
+    count = jnp.int32(0)
+    column = lax.broadcasted_iota(jnp.int32, list_ref.shape, 1)
+    listed = jnp.full(list_ref.shape, latest)
+    for place, there in enumerate(live):
+        value = jnp.where(there, place, latest)
+        order_ref[0, count] = value
+        listed = jnp.where(column == count, value, listed)
         count = count + there.astype(jnp.int32)
-
-    def fill(i, carry):
-        order_ref[i] = latest
-        return carry
-
-    lax.fori_loop(count, blocks * columns, fill, 0)
-    order_ref[blocks * columns] = count
+    order_ref[0, COUNT] = count
+    listed = jnp.where(column == COUNT, count, listed)
+    list_ref[...] = listed
 
     copies[2].wait()
     edge = width // 8 * 8
@@ -159,9 +167,15 @@
     out_ref[...] = jnp.broadcast_to(packed[...][None], out_ref.shape)
 
 
-def col_kernel(order_ref, scores_ref, lse_ref, log_ref, f_ref, out_ref, fcol, peak, total, packed, slot0, slot1):
+def col_kernel(
+    list_ref, scores_ref, lse_ref, log_ref, f_hbm, out_ref, order_ref, f_ref, fcol, peak, total, packed, slot0, slot1, sems
+):
+    listed = pltpu.make_async_copy(list_ref, order_ref, sems.at[0])
+    listed.start()
     f = EPS * log_ref[...] - EPS * logsum(lse_ref[...], 0)[0]
     f_ref[...] = f
+    kept = pltpu.make_async_copy(f_ref, f_hbm, sems.at[1])
+    kept.start()
     for k in range(f.shape[0]):
         row = jnp.broadcast_to(f[k : k + 1, :] * SCALE, (LANES, LANES))
         fcol[k * LANES : (k + 1) * LANES, :] = row.T
@@ -188,6 +202,7 @@
             sums[n % 2] = sums[n % 2] + jnp.sum(jnp.exp2(y - new[None]), axis=0)
         total[t] = sums[0] + sums[1]
 
+    listed.wait()
     slots = itertools.cycle((slot0, slot1))
     each(order_ref, columns, lambda tile: use(next(slots), tile))
     per_block = BLOCK // LANES
@@ -197,15 +212,20 @@
         for k, part in enumerate(lane_parts(safe_log(top, mass))):
             packed[t * per_block + k : t * per_block + k + 1, :] = part
     out_ref[...] = jnp.broadcast_to(packed[...][None], out_ref.shape)
+    kept.wait()
 
 
 def map_kernel(
-    order_ref, scores_ref, tgt_ref, lse_ref, log_ref, c_ref, out_ref,
-    crow, peak, denom, numer, buf, part0, part1,
+    list_ref, scores_ref, tgt_ref, lse_ref, log_ref, c_hbm, out_ref,
+    order_ref, c_ref, crow, peak, denom, numer, buf, part0, part1, sems,
 ):
     width = tgt_ref.shape[0]
+    listed = pltpu.make_async_copy(list_ref, order_ref, sems.at[0])
+    listed.start()
     c = EPS * log_ref[...] - EPS * logsum(lse_ref[...], 0)[0]
     c_ref[...] = c
+    kept = pltpu.make_async_copy(c_ref, c_hbm, sems.at[1])
+    kept.start()
     for k in range(c.shape[0]):
         crow[:, k * LANES : (k + 1) * LANES] = c[k : k + 1, :] * SCALE
     blocks, columns = peak.shape[0], tgt_ref.shape[1] // BLOCK
@@ -221,6 +241,7 @@
             values = scores_ref[place, at, :] * SCALE + own
             peak[b, at, :] = functools.reduce(jnp.maximum, lane_parts(values), peak[b, at, :])
 
+    listed.wait()
     each(order_ref, columns, first)
     tops = []
     for b in range(blocks):
@@ -245,7 +266,7 @@
         place, b, t, there = tile
         numer[b] = numer[b] + lax.dot_general(tgt_ref[:, block_of(t)], slots[n][...], NT, preferred_element_type=F32)
 
-    @pl.when(order_ref[order_ref.shape[0] - 1] > 0)
+    @pl.when(order_ref[0, COUNT] > 0)
     def _():
         in_turn(order_ref, columns, weigh, add)
 
@@ -263,6 +284,7 @@
             for r in range(BLOCK // chunk):
                 place = (b * (BLOCK // chunk) + r) * GROUPS + k
                 out_ref[place] = buf[:, r * chunk : (r + 1) * chunk].astype(BF16)
+    kept.wait()
 
 
 def merge_kernel(part, in_ref, out_ref, logs, buf):
@@ -299,7 +321,6 @@
 
 
 VMEM = pl.BlockSpec(memory_space=pltpu.VMEM)
-SMEM = pl.BlockSpec(memory_space=pltpu.SMEM)
 HBM = pl.BlockSpec(memory_space=pltpu.HBM)
 PARAMS = pltpu.CompilerParams(vmem_limit_bytes=24 * 1024 * 1024)
 
@@ -315,7 +336,7 @@
     )(*args)
 
 
-def run_rows(first, count, ids, src_t, tgt_t, g, log_src, log_tgt, n_tgt):
+def run_rows(count, ids, src_t, tgt_t, g, log_src, log_tgt, n_tgt):
     (width, s_rows), t_cols = src_t.shape, tgt_t.shape[1]
     blocks, columns = s_rows // BLOCK, t_cols // BLOCK
     padded = -(-width // LANES) * LANES
@@ -325,11 +346,12 @@
         (
             jax.ShapeDtypeStruct((blocks * columns, BLOCK, BLOCK), F32),
             jax.ShapeDtypeStruct((n_tgt, *s_tile), F32),
-            jax.ShapeDtypeStruct((blocks * columns + 1,), jnp.int32),
+            jax.ShapeDtypeStruct((1, LANES), jnp.int32),
             jax.ShapeDtypeStruct(log_src.shape, F32),
             jax.ShapeDtypeStruct(log_tgt.shape, F32),
         ),
         [
+            pltpu.SMEM((1, LANES), jnp.int32),
             pltpu.SMEM(count.shape, jnp.int32),
             pltpu.VMEM(ids.shape, jnp.int32),
             pltpu.VMEM(src_t.shape, BF16),
@@ -344,9 +366,8 @@
             pltpu.VMEM((BLOCK, BLOCK), F32),
             pltpu.SemaphoreType.DMA((7,)),
         ],
-        [SMEM] + [HBM] * 7,
-        first, *(pltpu.with_memory_space_constraint(x, pltpu.HBM) for x in (count, ids, src_t, tgt_t, g, log_src, log_tgt)),
-        outs=(VMEM, VMEM, SMEM, VMEM, VMEM),
+        [HBM] * 7,
+        *(pltpu.with_memory_space_constraint(x, pltpu.HBM) for x in (count, ids, src_t, tgt_t, g, log_src, log_tgt)),
     )
 
 
@@ -357,15 +378,19 @@
         col_kernel,
         (jax.ShapeDtypeStruct(s_tile, F32), jax.ShapeDtypeStruct((n_src, *t_tile), F32)),
         [
+            pltpu.SMEM((1, LANES), jnp.int32),
+            pltpu.VMEM(s_tile, F32),
             pltpu.VMEM((s_rows, LANES), F32),
             pltpu.VMEM((columns, 8, BLOCK), F32),
             pltpu.VMEM((columns, 8, BLOCK), F32),
             pltpu.VMEM(t_tile, F32),
             pltpu.VMEM((BLOCK, BLOCK), F32),
             pltpu.VMEM((BLOCK, BLOCK), F32),
+            pltpu.SemaphoreType.DMA((2,)),
         ],
-        [SMEM, VMEM, VMEM, VMEM],
+        [VMEM, VMEM, VMEM, VMEM],
         order, scores, lse, log_src,
+        outs=(HBM, VMEM),
     )
 
 
@@ -377,6 +402,8 @@
         map_kernel,
         (jax.ShapeDtypeStruct(t_tile, F32), jax.ShapeDtypeStruct((n_tgt, CHUNK, chunk), BF16)),
         [
+            pltpu.SMEM((1, LANES), jnp.int32),
+            pltpu.VMEM(t_tile, F32),
             pltpu.VMEM((1, t_cols), F32),
             pltpu.VMEM((blocks, BLOCK, LANES), F32),
             pltpu.VMEM((blocks, BLOCK, LANES), F32),
@@ -384,9 +411,11 @@
             pltpu.VMEM((CHUNK, BLOCK), F32),
             pltpu.VMEM((BLOCK, BLOCK), BF16),
             pltpu.VMEM((BLOCK, BLOCK), BF16),
+            pltpu.SemaphoreType.DMA((2,)),
         ],
-        [SMEM, VMEM, VMEM, VMEM, VMEM],
+        [VMEM, VMEM, VMEM, VMEM, VMEM],
         order, scores, tgt_t, lse, log_tgt,
+        outs=(HBM, VMEM),
     )
 
 
@@ -397,10 +426,9 @@
     src_t, tgt_t = src_emb.T, tgt_emb.T
     s_tile = (s_rows // LANES, LANES)
     t_tile = (t_cols // LANES, LANES)
-    first = (lax.axis_index("tgt") * (t_cols // BLOCK)).astype(jnp.int32).reshape(1)
 
     scores, lse, order, log_src, log_tgt = run_rows(
-        first, cand_count, cand_ids, src_t, tgt_t, g_init.reshape(1, t_cols),
+        cand_count, cand_ids, src_t, tgt_t, g_init.reshape(1, t_cols),
         log_src.reshape(s_tile), log_tgt.reshape(t_tile), n_tgt,
     )
     lse = lax.all_to_all(lse, "tgt", 0, 0, tiled=True)

time: 111 us -> 108 us (0.973)
  blocking collectives: 96.8 us -> 92 us
  Pallas kernels: 12.8 us -> 14 us
    all_to_all x1, blocking collectives: 26.6 us -> 22.9 us  [local(): lse = lax.all_to_all(lse, 'tgt', 0, 0, tiled=True)]
    pallas_call x5, Pallas kernels: 12.8 us -> 14 us  [call(): pl.pallas_call(kernel, out_shape=out_shape, in_specs=specs, out_specs=jax...]
    all_to_all x2, blocking collectives: 49.3 us -> 48.1 us  [local(): sums = lax.all_to_all(sums, 'tgt', 0, 0, tiled=True)]
where the time goes in v3:
time: 108 us; the launch traced here: 107 us
  blocking collectives  92 us (85%)
  Pallas kernels  14 us (13%)
    all_to_all x2, blocking collectives, local(): sums = lax.all_to_all(sums, 'tgt', 0, 0, tiled=True)  48.1 us
    all_to_all x1, blocking collectives, local(): lse = lax.all_to_all(lse, 'tgt', 0, 0, tiled=True)  22.9 us
    all_to_all x1, blocking collectives, local(): lse = lax.all_to_all(lse, 'src', 0, 0, tiled=True)  21 us
    pallas_call x5, Pallas kernels, call(): pl.pallas_call(kernel, out_shape=out_shape, in_specs=specs, out_specs=jax...  14 us

profile of v3, /device:TPU:1, one launch (start us, length us, event | category | flops | bytes accessed | tf_op | source)
XLA Modules:
  0.0 106.7 jit_solution(5376227510687748968)
XLA Ops:
  0.6 0.0 copy-start
  0.6 5.6 %shard_map.102 = (f32[16,512,512]{2,1,0:T(8,128)S(1)}, f32[32,8,128]{2,1,0:T(8,128)S(1)}, s32[1,128]{1,0:T(1,128)S(1)}, f32[8,128]{1,0:T(8,128)S(1)}, f32[32,128]{1,0:T(8,128)S(1)}) custom-call(s32[2]{0:T(128)} %count_hbm.1, s32[2,128]{1,0:T(2,128)} %ids_hbm.1, bf16[300,1024]{1,0:T(8,128)(2,1)} %bitcast.12, bf16[300,4096]{1,0:T(8,128)(2,1)} %bitcast.9, ...), custom_call_target="tpu_custom_call" | custom-call | tf_op jit(solution)/shard_map/pallas_call | solution.py:329
  6.3 22.9 %all_to_all.20.lse_ref = f32[32,8,128]{2,1,0:T(8,128)S(1)} all-to-all(f32[32,8,128]{2,1,0:T(8,128)S(1)} %get-tuple-element.17), channel_id=1, replica_groups=mesh['tgt'=32,'src'=16] {'tgt'}, dimensions={0} | all-to-all | bytes 262144 | tf_op jit(solution)/shard_map/all_to_all | solution.py:434
  29.1 2.3 %shard_map.103 = (f32[8,128]{1,0:T(8,128)}, f32[16,32,128]{2,1,0:T(8,128)S(1)}) custom-call(s32[1,128]{1,0:T(1,128)S(1)} %get-tuple-element.15.list_ref, f32[16,512,512]{2,1,0:T(8,128)S(1)} %get-tuple-element.16.scores_ref, f32[32,8,128]{2,1,0:T(8,128)S(1)} %all_to_all.20.lse_ref, f32[8,128]{1,0:T(8,128)S(1)} %get-tuple-element.18.log_ref), custom_call_target="tpu_custom_call" | custom-call | tf_op jit(solution)/shard_map/pallas_call | solution.py:329
  31.4 0.0 copy-start.1
  31.5 21.0 %all_to_all.21.lse_ref = f32[16,32,128]{2,1,0:T(8,128)S(1)} all-to-all(f32[16,32,128]{2,1,0:T(8,128)S(1)} %get-tuple-element.20), channel_id=1, replica_groups=mesh['tgt'=32,'src'=16] {'src'}, dimensions={0} | all-to-all | bytes 524288 | tf_op jit(solution)/shard_map/all_to_all | solution.py:436
  52.5 0.0 copy-done
  52.5 4.7 %shard_map.104 = (f32[32,128]{1,0:T(8,128)}, bf16[32,80,128]{2,1,0:T(8,128)(2,1)S(1)}) custom-call(s32[1,128]{1,0:T(1,128)S(1)} %get-tuple-element.15.list_ref, f32[16,512,512]{2,1,0:T(8,128)S(1)} %get-tuple-element.16.scores_ref, bf16[300,4096]{1,0:T(8,128)(2,1)S(1)} %bitcast.10, f32[16,32,128]{2,1,0:T(8,128)S(1)} %all_to_all.21.lse_ref, ...), custom_call_target="tpu_custom_call" | custom-call | tf_op jit(solution)/shard_map/pallas_call | solution.py:329
  57.2 24.9 %all_to_all.22.in_ref = bf16[32,80,128]{2,1,0:T(8,128)(2,1)S(1)} all-to-all(bf16[32,80,128]{2,1,0:T(8,128)(2,1)S(1)} %get-tuple-element.23), channel_id=1, replica_groups=mesh['tgt'=32,'src'=16] {'tgt'}, dimensions={0} | all-to-all | bytes 1310720 | tf_op jit(solution)/shard_map/all_to_all | solution.py:438
  82.1 0.2 shard_map.105
  82.4 23.2 %all_to_all.23.in_ref = bf16[32,80,128]{2,1,0:T(8,128)(2,1)S(1)} all-to-all(bf16[32,80,128]{2,1,0:T(8,128)(2,1)S(1)} %shard_map.105), channel_id=1, replica_groups=mesh['tgt'=32,'src'=16] {'tgt'}, dimensions={0} | all-to-all | bytes 1310720 | tf_op jit(solution)/shard_map/all_to_all | solution.py:447
  105.6 0.0 copy-done.1
  105.6 1.1 %shard_map.106 = (bf16[300,1024]{1,0:T(8,128)(2,1)}, f32[8,128]{1,0:T(8,128)}) custom-call(bf16[32,80,128]{2,1,0:T(8,128)(2,1)S(1)} %all_to_all.23.in_ref, f32[8,128]{1,0:T(8,128)S(1)} %copy-done.1), custom_call_target="tpu_custom_call" | custom-call | tf_op jit(solution)/shard_map/pallas_call | solution.py:329
Async XLA Ops:
  0.6 51.9 %copy-start = (bf16[4096,300]{0,1:T(8,128)(2,1)S(1)}, bf16[4096,300]{0,1:T(8,128)(2,1)}, u32[]{:S(2)}) copy-start(bf16[4096,300]{0,1:T(8,128)(2,1)} %param.8) | copy-start | bytes 7372804
  31.4 74.1 %copy-start.1 = (f32[8,128]{1,0:T(8,128)S(1)}, f32[8,128]{1,0:T(8,128)}, u32[]{:S(2)}) copy-start(f32[8,128]{1,0:T(8,128)} %get-tuple-element.19.f_ref) | copy-start | bytes 12292

commit v4 on v3

--- a/solution.py
+++ b/solution.py
@@ -16,6 +16,9 @@
 SCALE = INV / LN2
 STRIP = 32
 COUNT = 127
+BY_COLUMN = 64
+BY_ROW = 96
+TINY = 1e-27
 NEG = -1e30
 GROUPS = 4
 CHUNK = 80
@@ -124,6 +127,12 @@
         count = count + there.astype(jnp.int32)
     order_ref[0, COUNT] = count
     listed = jnp.where(column == COUNT, count, listed)
+    for t in range(columns):
+        there = functools.reduce(jnp.logical_or, live[t::columns])
+        listed = jnp.where(column == BY_COLUMN + t, there.astype(jnp.int32), listed)
+    for b in range(blocks):
+        there = functools.reduce(jnp.logical_or, live[b * columns : (b + 1) * columns])
+        listed = jnp.where(column == BY_ROW + b, there.astype(jnp.int32), listed)
     list_ref[...] = listed
 
     copies[2].wait()
@@ -167,8 +176,13 @@
     out_ref[...] = jnp.broadcast_to(packed[...][None], out_ref.shape)
 
 
+def too_small(order_ref, start, masses):
+    kept = [jnp.where(order_ref[0, start + i] > 0, mass, 1.0) for i, mass in enumerate(masses)]
+    return jnp.min(functools.reduce(jnp.minimum, kept)) < TINY
+
+
 def col_kernel(
-    list_ref, scores_ref, lse_ref, log_ref, f_hbm, out_ref, order_ref, f_ref, fcol, peak, total, packed, slot0, slot1, sems
+    list_ref, scores_ref, lse_ref, log_ref, f_hbm, fcol, out_ref, order_ref, f_ref, peak, total, packed, slot0, slot1, sems
 ):
     listed = pltpu.make_async_copy(list_ref, order_ref, sems.at[0])
     listed.start()
@@ -179,45 +193,70 @@
     for k in range(f.shape[0]):
         row = jnp.broadcast_to(f[k : k + 1, :] * SCALE, (LANES, LANES))
         fcol[k * LANES : (k + 1) * LANES, :] = row.T
-    peak[...] = jnp.full_like(peak, NEG)
     total[...] = jnp.zeros_like(total)
     columns = peak.shape[0]
-
-    def use(slot, tile):
+    per_block = BLOCK // LANES
+
+    def logits(tile, r):
         place, b, t, there = tile
         extra = jnp.where(there, 0.0, 2 * NEG)
-        old = peak[t]
-        tops = [old] * 2
-        for n, r in enumerate(range(0, BLOCK, STRIP)):
-            at = slice(r, r + STRIP)
-            own = fcol[pl.ds(pl.multiple_of(b * BLOCK + r, STRIP), STRIP), :] + extra
-            y = scores_ref[place, at, :] * SCALE + jnp.concatenate([own] * (BLOCK // LANES), axis=1)
-            slot[at, :] = y
-            tops[n % 2] = jnp.maximum(tops[n % 2], jnp.max(y.reshape(STRIP // 8, 8, BLOCK), axis=0))
-        new = jnp.maximum(*tops)
-        peak[t] = new
-        sums = [total[t] * jnp.exp2(old - new), jnp.zeros_like(new)]
-        for n, r in enumerate(range(0, BLOCK, STRIP)):
-            y = slot[slice(r, r + STRIP), :].reshape(STRIP // 8, 8, BLOCK)
-            sums[n % 2] = sums[n % 2] + jnp.sum(jnp.exp2(y - new[None]), axis=0)
-        total[t] = sums[0] + sums[1]
+        own = fcol[pl.ds(pl.multiple_of(b * BLOCK + r, STRIP), STRIP), :] + extra
+        return scores_ref[place, r : r + STRIP, :] * SCALE + jnp.concatenate([own] * per_block, axis=1)
+
+    def by_eight(values):
+        return values.reshape(STRIP // 8, 8, BLOCK)
+
+    def use(tile):
+        sums = [total[tile[2]], jnp.zeros((8, BLOCK), F32)]
+        for i, r in enumerate(range(0, BLOCK, STRIP)):
+            sums[i % 2] = sums[i % 2] + jnp.sum(by_eight(jnp.exp2(logits(tile, r))), axis=0)
+        total[tile[2]] = sums[0] + sums[1]
 
     listed.wait()
-    slots = itertools.cycle((slot0, slot1))
-    each(order_ref, columns, lambda tile: use(next(slots), tile))
-    per_block = BLOCK // LANES
-    for t in range(columns):
-        top = jnp.max(peak[t], axis=0, keepdims=True)
-        mass = jnp.sum(total[t] * jnp.exp2(peak[t] - top), axis=0, keepdims=True)
+    each(order_ref, columns, use)
+
+    def pack(t, top, mass):
         for k, part in enumerate(lane_parts(safe_log(top, mass))):
             packed[t * per_block + k : t * per_block + k + 1, :] = part
+
+    masses = [jnp.sum(total[t], axis=0, keepdims=True) for t in range(columns)]
+    for t in range(columns):
+        pack(t, 0.0, masses[t])
+
+    @pl.when(too_small(order_ref, BY_COLUMN, masses))
+    def _():
+        peak[...] = jnp.full_like(peak, NEG)
+        total[...] = jnp.zeros_like(total)
+
+        def scaled(slot, tile):
+            t = tile[2]
+            old = peak[t]
+            tops = [old] * 2
+            for i, r in enumerate(range(0, BLOCK, STRIP)):
+                y = logits(tile, r)
+                slot[r : r + STRIP, :] = y
+                tops[i % 2] = jnp.maximum(tops[i % 2], jnp.max(by_eight(y), axis=0))
+            new = jnp.maximum(*tops)
+            peak[t] = new
+            sums = [total[t] * jnp.exp2(old - new), jnp.zeros_like(new)]
+            for i, r in enumerate(range(0, BLOCK, STRIP)):
+                y = by_eight(slot[r : r + STRIP, :])
+                sums[i % 2] = sums[i % 2] + jnp.sum(jnp.exp2(y - new[None]), axis=0)
+            total[t] = sums[0] + sums[1]
+
+        slots = itertools.cycle((slot0, slot1))
+        each(order_ref, columns, lambda tile: scaled(next(slots), tile))
+        for t in range(columns):
+            top = jnp.max(peak[t], axis=0, keepdims=True)
+            pack(t, top, jnp.sum(total[t] * jnp.exp2(peak[t] - top), axis=0, keepdims=True))
+
     out_ref[...] = jnp.broadcast_to(packed[...][None], out_ref.shape)
     kept.wait()
 
 
 def map_kernel(
-    list_ref, scores_ref, tgt_ref, lse_ref, log_ref, c_hbm, out_ref,
-    order_ref, c_ref, crow, peak, denom, numer, buf, part0, part1, sems,
+    list_ref, scores_ref, tgt_ref, lse_ref, log_ref, fcol, c_hbm, out_ref,
+    order_ref, c_ref, crow, peak, shift, tops, denom, numer, buf, part0, part1, sems,
 ):
     width = tgt_ref.shape[0]
     listed = pltpu.make_async_copy(list_ref, order_ref, sems.at[0])
@@ -229,36 +268,20 @@
     for k in range(c.shape[0]):
         crow[:, k * LANES : (k + 1) * LANES] = c[k : k + 1, :] * SCALE
     blocks, columns = peak.shape[0], tgt_ref.shape[1] // BLOCK
-    peak[...] = jnp.full_like(peak, NEG)
-    denom[...] = jnp.zeros_like(denom)
-    numer[...] = jnp.zeros_like(numer)
-
-    def first(tile):
+    slots = (part0, part1)
+
+    def strip(b, r):
+        return pl.ds(pl.multiple_of(b * BLOCK + r, STRIP), STRIP)
+
+    def weigh(shift_ref, n, tile):
         place, b, t, there = tile
+        extra = jnp.where(there, 0.0, 2 * NEG)
         own = crow[:, block_of(t)]
         for r in range(0, BLOCK, STRIP):
             at = slice(r, r + STRIP)
+            moved = shift_ref[strip(b, r), :] + extra
             values = scores_ref[place, at, :] * SCALE + own
-            peak[b, at, :] = functools.reduce(jnp.maximum, lane_parts(values), peak[b, at, :])
-
-    listed.wait()
-    each(order_ref, columns, first)
-    tops = []
-    for b in range(blocks):
-        tops.append(jnp.max(peak[b].T, axis=0, keepdims=True))
-        peak[b] = jnp.broadcast_to(jnp.max(peak[b], axis=1, keepdims=True), peak[b].shape)
-
-    slots = (part0, part1)
-
-    def weigh(n, tile):
-        place, b, t, there = tile
-        extra = jnp.where(there, 0.0, -NEG)
-        own = crow[:, block_of(t)]
-        for r in range(0, BLOCK, STRIP):
-            at = slice(r, r + STRIP)
-            top = peak[b, at, :] + extra
-            values = scores_ref[place, at, :] * SCALE + own
-            weights = [jnp.exp2(part - top).astype(BF16) for part in lane_parts(values)]
+            weights = [jnp.exp2(part + moved).astype(BF16) for part in lane_parts(values)]
             slots[n][at, :] = jnp.concatenate(weights, axis=1)
             denom[b, at, :] = denom[b, at, :] + sum(part.astype(F32) for part in weights)
 
@@ -266,16 +289,45 @@
         place, b, t, there = tile
         numer[b] = numer[b] + lax.dot_general(tgt_ref[:, block_of(t)], slots[n][...], NT, preferred_element_type=F32)
 
-    @pl.when(order_ref[0, COUNT] > 0)
+    def totals(shift_ref):
+        denom[...] = jnp.zeros_like(denom)
+        numer[...] = jnp.zeros_like(numer)
+
+        @pl.when(order_ref[0, COUNT] > 0)
+        def _():
+            in_turn(order_ref, columns, functools.partial(weigh, shift_ref), add)
+
+    def masses():
+        return [jnp.sum(denom[b].T, axis=0, keepdims=True) for b in range(blocks)]
+
+    tops[...] = jnp.zeros_like(tops)
+    listed.wait()
+    totals(fcol)
+
+    @pl.when(too_small(order_ref, BY_ROW, masses()))
     def _():
-        in_turn(order_ref, columns, weigh, add)
+        peak[...] = jnp.full_like(peak, NEG)
+
+        def first(tile):
+            place, b, t, there = tile
+            own = crow[:, block_of(t)]
+            for r in range(0, BLOCK, STRIP):
+                at = slice(r, r + STRIP)
+                parts = [part + fcol[strip(b, r), :] for part in lane_parts(scores_ref[place, at, :] * SCALE + own)]
+                peak[b, at, :] = functools.reduce(jnp.maximum, parts, peak[b, at, :])
+
+        each(order_ref, columns, first)
+        for b in range(blocks):
+            rows = slice(b * BLOCK, (b + 1) * BLOCK)
+            tops[b : b + 1, :] = jnp.max(peak[b].T, axis=0, keepdims=True)
+            shift[rows, :] = fcol[rows, :] - jnp.max(peak[b], axis=1, keepdims=True)
+        totals(shift)
 
     part = width // GROUPS
     chunk = out_ref.shape[2]
-    for b in range(blocks):
-        mass = jnp.sum(denom[b].T, axis=0, keepdims=True)
+    for b, mass in enumerate(masses()):
         inverse = 1.0 / jnp.where(mass > 0.0, mass, 1.0)
-        logs = three_parts(safe_log(tops[b], mass))
+        logs = three_parts(safe_log(tops[b : b + 1, :], mass))
         for k in range(GROUPS):
             buf[:part, :] = numer[b, k * part : (k + 1) * part, :] * inverse
             for j in range(3):
@@ -305,19 +357,26 @@
     out_ref[...] = jnp.broadcast_to(buf[...].astype(BF16)[None], out_ref.shape)
 
 
-def final_kernel(part, in_ref, f_ref, mapped_ref, mass_ref, buf):
+def final_kernel(part, in_ref, mapped_hbm, mass_ref, mapped, buf, sems):
     chunk = in_ref.shape[2]
     per = chunk // LANES
-    for r in range(in_ref.shape[0] // GROUPS):
+    count = in_ref.shape[0] // GROUPS
+    copies = []
+    for r in range(count):
         for k in range(GROUPS):
             piece = in_ref[r * GROUPS + k].astype(F32)
             buf[k * part : (k + 1) * part, :] = piece[:part]
-        mapped_ref[:, r * chunk : (r + 1) * chunk] = buf[: GROUPS * part, :].astype(BF16)
+        mapped[:, r * chunk : (r + 1) * chunk] = buf[: GROUPS * part, :].astype(BF16)
         total = piece[part : part + 1] + piece[part + 1 : part + 2] + piece[part + 2 : part + 3]
         for j in range(per):
-            at = r * per + j
-            own = f_ref[at : at + 1, :] * INV
-            mass_ref[at : at + 1, :] = own + total[:, j * LANES : (j + 1) * LANES]
+            mass_ref[r * per + j : r * per + j + 1, :] = total[:, j * LANES : (j + 1) * LANES]
+        if (r + 1) % (count // 2) == 0:
+            n = len(copies)
+            half = pl.ds(n * (count // 2) * chunk, (count // 2) * chunk)
+            copies.append(pltpu.make_async_copy(mapped.at[:, half], mapped_hbm.at[:, half], sems.at[n]))
+            copies[n].start()
+    for copy in copies:
+        copy.wait()
 
 
 VMEM = pl.BlockSpec(memory_space=pltpu.VMEM)
@@ -376,11 +435,14 @@
     t_tile, columns = (t_cols // LANES, LANES), t_cols // BLOCK
     return call(
         col_kernel,
-        (jax.ShapeDtypeStruct(s_tile, F32), jax.ShapeDtypeStruct((n_src, *t_tile), F32)),
+        (
+            jax.ShapeDtypeStruct(s_tile, F32),
+            jax.ShapeDtypeStruct((s_rows, LANES), F32),
+            jax.ShapeDtypeStruct((n_src, *t_tile), F32),
+        ),
         [
             pltpu.SMEM((1, LANES), jnp.int32),
             pltpu.VMEM(s_tile, F32),
-            pltpu.VMEM((s_rows, LANES), F32),
             pltpu.VMEM((columns, 8, BLOCK), F32),
             pltpu.VMEM((columns, 8, BLOCK), F32),
             pltpu.VMEM(t_tile, F32),
@@ -390,11 +452,12 @@
         ],
         [VMEM, VMEM, VMEM, VMEM],
         order, scores, lse, log_src,
-        outs=(HBM, VMEM),
-    )
-
-
-def run_map(order, scores, tgt_t, lse, log_tgt, n_tgt, s_rows):
+        outs=(HBM, VMEM, VMEM),
+    )
+
+
+def run_map(order, scores, tgt_t, lse, log_tgt, fcol, n_tgt):
+    s_rows = fcol.shape[0]
     t_tile, (width, t_cols) = log_tgt.shape, tgt_t.shape
     blocks, columns = s_rows // BLOCK, t_cols // BLOCK
     chunk = s_rows * GROUPS // n_tgt
@@ -406,6 +469,8 @@
             pltpu.VMEM(t_tile, F32),
             pltpu.VMEM((1, t_cols), F32),
             pltpu.VMEM((blocks, BLOCK, LANES), F32),
+            pltpu.VMEM(fcol.shape, F32),
+            pltpu.VMEM((blocks, BLOCK), F32),
             pltpu.VMEM((blocks, BLOCK, LANES), F32),
             pltpu.VMEM((blocks, width, BLOCK), F32),
             pltpu.VMEM((CHUNK, BLOCK), F32),
@@ -413,8 +478,8 @@
             pltpu.VMEM((BLOCK, BLOCK), BF16),
             pltpu.SemaphoreType.DMA((2,)),
         ],
-        [VMEM, VMEM, VMEM, VMEM, VMEM],
-        order, scores, tgt_t, lse, log_tgt,
+        [VMEM] * 6,
+        order, scores, tgt_t, lse, log_tgt, fcol,
         outs=(HBM, VMEM),
     )
 
@@ -432,9 +497,9 @@
         log_src.reshape(s_tile), log_tgt.reshape(t_tile), n_tgt,
     )
     lse = lax.all_to_all(lse, "tgt", 0, 0, tiled=True)
-    f, lse = run_cols(order, scores, lse, log_src, n_src, t_cols)
+    f, fcol, lse = run_cols(order, scores, lse, log_src, n_src, t_cols)
     lse = lax.all_to_all(lse, "src", 0, 0, tiled=True)
-    c, sums = run_map(order, scores, tgt_t, lse, log_tgt, n_tgt, s_rows)
+    c, sums = run_map(order, scores, tgt_t, lse, log_tgt, fcol, n_tgt)
     sums = lax.all_to_all(sums, "tgt", 0, 0, tiled=True)
     part, chunk = width // GROUPS, sums.shape[2]
     sums = call(
@@ -448,9 +513,14 @@
     mapped, mass = call(
         functools.partial(final_kernel, part),
         (jax.ShapeDtypeStruct((width, s_rows), BF16), jax.ShapeDtypeStruct(s_tile, F32)),
-        [pltpu.VMEM((-(-width // 8) * 8, chunk), F32)],
-        [VMEM, VMEM],
-        sums, f,
+        [
+            pltpu.VMEM((width, s_rows), BF16),
+            pltpu.VMEM((-(-width // 8) * 8, chunk), F32),
+            pltpu.SemaphoreType.DMA((2,)),
+        ],
+        [VMEM],
+        sums,
+        outs=(HBM, VMEM),
     )
     return f.reshape(s_rows), c.reshape(t_cols), mapped.T, mass.reshape(s_rows)
 

time: 108 us -> 112 us (1.037)
  the two profiles are of different devices: /device:TPU:1 before, /device:TPU:8 now
where the time goes in v4:
time: 112 us; the launch traced here: 111 us
  blocking collectives  89.3 us (80%)
  Pallas kernels  21.3 us (19%)
    all_to_all x2, blocking collectives, local(): sums = lax.all_to_all(sums, 'tgt', 0, 0, tiled=True)  49.3 us
    all_to_all x1, blocking collectives, local(): lse = lax.all_to_all(lse, 'tgt', 0, 0, tiled=True)  23.5 us
    pallas_call x5, Pallas kernels, call(): pl.pallas_call(kernel, out_shape=out_shape, in_specs=specs, out_specs=jax...  21.3 us
    all_to_all x1, blocking collectives, local(): lse = lax.all_to_all(lse, 'src', 0, 0, tiled=True)  16.5 us

profile of v4, /device:TPU:8, one launch (start us, length us, event | category | flops | bytes accessed | tf_op | source)
XLA Modules:
  0.0 111.3 jit_solution(9827368579868299918)
XLA Ops:
  0.6 0.0 copy-start
  0.6 6.5 %shard_map.102 = (f32[16,512,512]{2,1,0:T(8,128)S(1)}, f32[32,8,128]{2,1,0:T(8,128)S(1)}, s32[1,128]{1,0:T(1,128)S(1)}, f32[8,128]{1,0:T(8,128)S(1)}, f32[32,128]{1,0:T(8,128)S(1)}) custom-call(s32[2]{0:T(128)} %count_hbm.1, s32[2,128]{1,0:T(2,128)} %ids_hbm.1, bf16[300,1024]{1,0:T(8,128)(2,1)} %bitcast.11, bf16[300,4096]{1,0:T(8,128)(2,1)} %bitcast.9, ...), custom_call_target="tpu_custom_call" | custom-call | tf_op jit(solution)/shard_map/pallas_call | solution.py:388
  7.2 23.5 %all_to_all.20.lse_ref = f32[32,8,128]{2,1,0:T(8,128)S(1)} all-to-all(f32[32,8,128]{2,1,0:T(8,128)S(1)} %get-tuple-element.18), channel_id=1, replica_groups=mesh['tgt'=32,'src'=16] {'tgt'}, dimensions={0} | all-to-all | bytes 262144 | tf_op jit(solution)/shard_map/all_to_all | solution.py:499
  30.7 2.0 %shard_map.103 = (f32[8,128]{1,0:T(8,128)}, f32[1024,128]{1,0:T(8,128)S(1)}, f32[16,32,128]{2,1,0:T(8,128)S(1)}) custom-call(s32[1,128]{1,0:T(1,128)S(1)} %get-tuple-element.16.list_ref, f32[16,512,512]{2,1,0:T(8,128)S(1)} %get-tuple-element.17.scores_ref, f32[32,8,128]{2,1,0:T(8,128)S(1)} %all_to_all.20.lse_ref, f32[8,128]{1,0:T(8,128)S(1)} %get-tuple-element.19.log_ref), custom_call_target="tpu_custom_call" | custom-call | tf_op jit(solution)/shard_map/pallas_call | solution.py:388
  32.7 16.5 %all_to_all.21.lse_ref = f32[16,32,128]{2,1,0:T(8,128)S(1)} all-to-all(f32[16,32,128]{2,1,0:T(8,128)S(1)} %get-tuple-element.21), channel_id=1, replica_groups=mesh['tgt'=32,'src'=16] {'src'}, dimensions={0} | all-to-all | bytes 524288 | tf_op jit(solution)/shard_map/all_to_all | solution.py:501
  49.1 0.0 copy-done
  49.1 11.0 %shard_map.104 = (f32[32,128]{1,0:T(8,128)}, bf16[32,80,128]{2,1,0:T(8,128)(2,1)S(1)}) custom-call(s32[1,128]{1,0:T(1,128)S(1)} %get-tuple-element.16.list_ref, f32[16,512,512]{2,1,0:T(8,128)S(1)} %get-tuple-element.17.scores_ref, bf16[300,4096]{1,0:T(8,128)(2,1)S(1)} %bitcast.10, f32[16,32,128]{2,1,0:T(8,128)S(1)} %all_to_all.21.lse_ref, ...), custom_call_target="tpu_custom_call" | custom-call | tf_op jit(solution)/shard_map/pallas_call | solution.py:388
  60.1 25.1 %all_to_all.22.in_ref = bf16[32,80,128]{2,1,0:T(8,128)(2,1)S(1)} all-to-all(bf16[32,80,128]{2,1,0:T(8,128)(2,1)S(1)} %get-tuple-element.25), channel_id=1, replica_groups=mesh['tgt'=32,'src'=16] {'tgt'}, dimensions={0} | all-to-all | bytes 1310720 | tf_op jit(solution)/shard_map/all_to_all | solution.py:503
  85.3 0.2 shard_map.105
  85.5 24.2 %all_to_all.23.in_ref = bf16[32,80,128]{2,1,0:T(8,128)(2,1)S(1)} all-to-all(bf16[32,80,128]{2,1,0:T(8,128)(2,1)S(1)} %shard_map.105), channel_id=1, replica_groups=mesh['tgt'=32,'src'=16] {'tgt'}, dimensions={0} | all-to-all | bytes 1310720 | tf_op jit(solution)/shard_map/all_to_all | solution.py:512
  109.7 1.6 %shard_map.106 = (bf16[300,1024]{1,0:T(8,128)(2,1)}, f32[8,128]{1,0:T(8,128)}) custom-call(bf16[32,80,128]{2,1,0:T(8,128)(2,1)S(1)} %all_to_all.23.in_ref), custom_call_target="tpu_custom_call" | custom-call | tf_op jit(solution)/shard_map/pallas_call | solution.py:388
Async XLA Ops:
  0.6 48.5 %copy-start = (bf16[4096,300]{0,1:T(8,128)(2,1)S(1)}, bf16[4096,300]{0,1:T(8,128)(2,1)}, u32[]{:S(2)}) copy-start(bf16[4096,300]{0,1:T(8,128)(2,1)} %param.8) | copy-start | bytes 7372804

commit v5 on v4

--- a/solution.py
+++ b/solution.py
@@ -15,6 +15,7 @@
 LN2 = 0.6931471805599453
 SCALE = INV / LN2
 STRIP = 32
+PART = 512
 COUNT = 127
 BY_COLUMN = 64
 BY_ROW = 96
@@ -54,14 +55,18 @@
 
 def in_turn(order_ref, columns, make, use):
     tile = functools.partial(pick, order_ref, columns=columns)
-    make(0, tile(0))
+    starts = range(0, BLOCK, PART)
+    for start in starts:
+        make(0, tile(0), start)
 
     def step(k, carry):
         i = 2 * k
-        make(1, tile(i + 1))
-        use(0, tile(i))
-        make(0, tile(i + 2))
-        use(1, tile(i + 1))
+        for start in starts:
+            make(1, tile(i + 1), start)
+            use(0, tile(i), start)
+        for start in starts:
+            make(0, tile(i + 2), start)
+            use(1, tile(i + 1), start)
         return carry
 
     lax.fori_loop(0, (order_ref[0, COUNT] + 1) // 2, step, 0)
@@ -147,19 +152,20 @@
 
     slots = (slot0, slot1)
 
-    def make(n, tile):
+    def make(n, tile, start):
         place, b, t, there = tile
-        rows = rows_ref[block_of(b), :]
-        slots[n][...] = jnp.dot(rows[:, :width], tgt_ref[:, block_of(t)], preferred_element_type=F32)
-
-    def use(n, tile):
+        at = slice(start, start + PART)
+        rows = rows_ref[pl.ds(pl.multiple_of(b * BLOCK + start, PART), PART), :]
+        values = jnp.dot(rows[:, :width], tgt_ref[:, block_of(t)], preferred_element_type=F32)
+        slots[n][at, :] = values
+        scores_ref[place, at, :] = values
+
+    def use(n, tile, start):
         place, b, t, there = tile
         g = jnp.where(there, g_ref[:, block_of(t)] * SCALE, 2 * NEG)
-        for r in range(0, BLOCK, STRIP):
+        for r in range(start, start + PART, STRIP):
             at = slice(r, r + STRIP)
-            values = slots[n][at, :]
-            scores_ref[place, at, :] = values
-            z = lane_parts(values * SCALE + g)
+            z = lane_parts(slots[n][at, :] * SCALE + g)
             old = peak[b, at, :]
             new = functools.reduce(jnp.maximum, z, old)
             peak[b, at, :] = new
@@ -273,11 +279,11 @@
     def strip(b, r):
         return pl.ds(pl.multiple_of(b * BLOCK + r, STRIP), STRIP)
 
-    def weigh(shift_ref, n, tile):
+    def weigh(shift_ref, n, tile, start):
         place, b, t, there = tile
         extra = jnp.where(there, 0.0, 2 * NEG)
         own = crow[:, block_of(t)]
-        for r in range(0, BLOCK, STRIP):
+        for r in range(start, start + PART, STRIP):
             at = slice(r, r + STRIP)
             moved = shift_ref[strip(b, r), :] + extra
             values = scores_ref[place, at, :] * SCALE + own
@@ -285,9 +291,12 @@
             slots[n][at, :] = jnp.concatenate(weights, axis=1)
             denom[b, at, :] = denom[b, at, :] + sum(part.astype(F32) for part in weights)
 
-    def add(n, tile):
+    def add(n, tile, start):
         place, b, t, there = tile
-        numer[b] = numer[b] + lax.dot_general(tgt_ref[:, block_of(t)], slots[n][...], NT, preferred_element_type=F32)
+        at = slice(start, start + PART)
+        numer[b, :, at] = numer[b, :, at] + lax.dot_general(
+            tgt_ref[:, block_of(t)], slots[n][at, :], NT, preferred_element_type=F32
+        )
 
     def totals(shift_ref):
         denom[...] = jnp.zeros_like(denom)
@@ -357,26 +366,17 @@
     out_ref[...] = jnp.broadcast_to(buf[...].astype(BF16)[None], out_ref.shape)
 
 
-def final_kernel(part, in_ref, mapped_hbm, mass_ref, mapped, buf, sems):
+def final_kernel(part, in_ref, mapped_ref, mass_ref, buf):
     chunk = in_ref.shape[2]
     per = chunk // LANES
-    count = in_ref.shape[0] // GROUPS
-    copies = []
-    for r in range(count):
+    for r in range(in_ref.shape[0] // GROUPS):
         for k in range(GROUPS):
             piece = in_ref[r * GROUPS + k].astype(F32)
             buf[k * part : (k + 1) * part, :] = piece[:part]
-        mapped[:, r * chunk : (r + 1) * chunk] = buf[: GROUPS * part, :].astype(BF16)
+        mapped_ref[:, r * chunk : (r + 1) * chunk] = buf[: GROUPS * part, :].astype(BF16)
         total = piece[part : part + 1] + piece[part + 1 : part + 2] + piece[part + 2 : part + 3]
         for j in range(per):
             mass_ref[r * per + j : r * per + j + 1, :] = total[:, j * LANES : (j + 1) * LANES]
-        if (r + 1) % (count // 2) == 0:
-            n = len(copies)
-            half = pl.ds(n * (count // 2) * chunk, (count // 2) * chunk)
-            copies.append(pltpu.make_async_copy(mapped.at[:, half], mapped_hbm.at[:, half], sems.at[n]))
-            copies[n].start()
-    for copy in copies:
-        copy.wait()
 
 
 VMEM = pl.BlockSpec(memory_space=pltpu.VMEM)
@@ -513,14 +513,9 @@
     mapped, mass = call(
         functools.partial(final_kernel, part),
         (jax.ShapeDtypeStruct((width, s_rows), BF16), jax.ShapeDtypeStruct(s_tile, F32)),
-        [
-            pltpu.VMEM((width, s_rows), BF16),
-            pltpu.VMEM((-(-width // 8) * 8, chunk), F32),
-            pltpu.SemaphoreType.DMA((2,)),
-        ],
+        [pltpu.VMEM((-(-width // 8) * 8, chunk), F32)],
         [VMEM],
         sums,
-        outs=(HBM, VMEM),
     )
     return f.reshape(s_rows), c.reshape(t_cols), mapped.T, mass.reshape(s_rows)
 

time: 112 us -> 110 us (0.982)
  the two profiles are of different devices: /device:TPU:8 before, /device:TPU:1 now
where the time goes in v5:
time: 110 us; the launch traced here: 108 us
  blocking collectives  93.5 us (85%)
  Pallas kernels  13.9 us (13%)
    all_to_all x2, blocking collectives, local(): sums = lax.all_to_all(sums, 'tgt', 0, 0, tiled=True)  49.4 us
    all_to_all x1, blocking collectives, local(): lse = lax.all_to_all(lse, 'tgt', 0, 0, tiled=True)  24.4 us
    all_to_all x1, blocking collectives, local(): lse = lax.all_to_all(lse, 'src', 0, 0, tiled=True)  19.7 us
    pallas_call x5, Pallas kernels, call(): pl.pallas_call(kernel, out_shape=out_shape, in_specs=specs, out_specs=jax...  13.9 us

profile of v5, /device:TPU:1, one launch (start us, length us, event | category | flops | bytes accessed | tf_op | source)
XLA Modules:
  0.0 108.0 jit_solution(9382639616834477397)
XLA Ops:
  0.6 0.0 copy-start
  0.6 4.5 %shard_map.102 = (f32[16,512,512]{2,1,0:T(8,128)S(1)}, f32[32,8,128]{2,1,0:T(8,128)S(1)}, s32[1,128]{1,0:T(1,128)S(1)}, f32[8,128]{1,0:T(8,128)S(1)}, f32[32,128]{1,0:T(8,128)S(1)}) custom-call(s32[2]{0:T(128)} %count_hbm.1, s32[2,128]{1,0:T(2,128)} %ids_hbm.1, bf16[300,1024]{1,0:T(8,128)(2,1)} %bitcast.11, bf16[300,4096]{1,0:T(8,128)(2,1)} %bitcast.9, ...), custom_call_target="tpu_custom_call" | custom-call | tf_op jit(solution)/shard_map/pallas_call | solution.py:388
  5.1 24.4 %all_to_all.20.lse_ref = f32[32,8,128]{2,1,0:T(8,128)S(1)} all-to-all(f32[32,8,128]{2,1,0:T(8,128)S(1)} %get-tuple-element.18), channel_id=1, replica_groups=mesh['tgt'=32,'src'=16] {'tgt'}, dimensions={0} | all-to-all | bytes 262144 | tf_op jit(solution)/shard_map/all_to_all | solution.py:499
  29.5 1.4 %shard_map.103 = (f32[8,128]{1,0:T(8,128)}, f32[1024,128]{1,0:T(8,128)S(1)}, f32[16,32,128]{2,1,0:T(8,128)S(1)}) custom-call(s32[1,128]{1,0:T(1,128)S(1)} %get-tuple-element.16.list_ref, f32[16,512,512]{2,1,0:T(8,128)S(1)} %get-tuple-element.17.scores_ref, f32[32,8,128]{2,1,0:T(8,128)S(1)} %all_to_all.20.lse_ref, f32[8,128]{1,0:T(8,128)S(1)} %get-tuple-element.19.log_ref), custom_call_target="tpu_custom_call" | custom-call | tf_op jit(solution)/shard_map/pallas_call | solution.py:388
  31.0 19.7 %all_to_all.21.lse_ref = f32[16,32,128]{2,1,0:T(8,128)S(1)} all-to-all(f32[16,32,128]{2,1,0:T(8,128)S(1)} %get-tuple-element.21), channel_id=1, replica_groups=mesh['tgt'=32,'src'=16] {'src'}, dimensions={0} | all-to-all | bytes 524288 | tf_op jit(solution)/shard_map/all_to_all | solution.py:501
  50.6 0.0 copy-done
  50.6 6.6 %shard_map.104 = (f32[32,128]{1,0:T(8,128)}, bf16[32,80,128]{2,1,0:T(8,128)(2,1)S(1)}) custom-call(s32[1,128]{1,0:T(1,128)S(1)} %get-tuple-element.16.list_ref, f32[16,512,512]{2,1,0:T(8,128)S(1)} %get-tuple-element.17.scores_ref, bf16[300,4096]{1,0:T(8,128)(2,1)S(1)} %bitcast.10, f32[16,32,128]{2,1,0:T(8,128)S(1)} %all_to_all.21.lse_ref, ...), custom_call_target="tpu_custom_call" | custom-call | tf_op jit(solution)/shard_map/pallas_call | solution.py:388
  57.3 26.5 %all_to_all.22.in_ref = bf16[32,80,128]{2,1,0:T(8,128)(2,1)S(1)} all-to-all(bf16[32,80,128]{2,1,0:T(8,128)(2,1)S(1)} %get-tuple-element.25), channel_id=1, replica_groups=mesh['tgt'=32,'src'=16] {'tgt'}, dimensions={0} | all-to-all | bytes 1310720 | tf_op jit(solution)/shard_map/all_to_all | solution.py:503
  83.8 0.2 shard_map.105
  84.0 22.9 %all_to_all.23.in_ref = bf16[32,80,128]{2,1,0:T(8,128)(2,1)S(1)} all-to-all(bf16[32,80,128]{2,1,0:T(8,128)(2,1)S(1)} %shard_map.105), channel_id=1, replica_groups=mesh['tgt'=32,'src'=16] {'tgt'}, dimensions={0} | all-to-all | bytes 1310720 | tf_op jit(solution)/shard_map/all_to_all | solution.py:512
  106.9 1.1 shard_map.106
Async XLA Ops:
  0.6 50.0 %copy-start = (bf16[4096,300]{0,1:T(8,128)(2,1)S(1)}, bf16[4096,300]{0,1:T(8,128)(2,1)}, u32[]{:S(2)}) copy-start(bf16[4096,300]{0,1:T(8,128)(2,1)} %param.8) | copy-start | bytes 7372804

commit v6 on v5

--- a/solution.py
+++ b/solution.py
@@ -120,7 +120,7 @@
     latest = jnp.int32(0)
     for place, there in enumerate(live):
         latest = jnp.where(there, place, latest)
-    for i in range(len(live)):
+    for i in range(len(live) + 2):
         order_ref[0, i] = latest
     count = jnp.int32(0)
     column = lax.broadcasted_iota(jnp.int32, list_ref.shape, 1)
@@ -262,7 +262,7 @@
 
 def map_kernel(
     list_ref, scores_ref, tgt_ref, lse_ref, log_ref, fcol, c_hbm, out_ref,
-    order_ref, c_ref, crow, peak, shift, tops, denom, numer, buf, part0, part1, sems,
+    order_ref, c_ref, crow, peak, shift, tops, mass_ref, denom, numer, buf, part0, part1, sems,
 ):
     width = tgt_ref.shape[0]
     listed = pltpu.make_async_copy(list_ref, order_ref, sems.at[0])
@@ -306,8 +306,11 @@
         def _():
             in_turn(order_ref, columns, functools.partial(weigh, shift_ref), add)
 
+        for b in range(blocks):
+            mass_ref[b : b + 1, :] = jnp.sum(denom[b].T, axis=0, keepdims=True)
+
     def masses():
-        return [jnp.sum(denom[b].T, axis=0, keepdims=True) for b in range(blocks)]
+        return [mass_ref[b : b + 1, :] for b in range(blocks)]
 
     tops[...] = jnp.zeros_like(tops)
     listed.wait()
@@ -471,6 +474,7 @@
             pltpu.VMEM((blocks, BLOCK, LANES), F32),
             pltpu.VMEM(fcol.shape, F32),
             pltpu.VMEM((blocks, BLOCK), F32),
+            pltpu.VMEM((blocks, BLOCK), F32),
             pltpu.VMEM((blocks, BLOCK, LANES), F32),
             pltpu.VMEM((blocks, width, BLOCK), F32),
             pltpu.VMEM((CHUNK, BLOCK), F32),

time: 110 us -> 112 us (1.018)
  blocking collectives: 93.5 us -> 95.1 us
    all_to_all x1, blocking collectives: 24.4 us -> 26.1 us  [local(): lse = lax.all_to_all(lse, 'tgt', 0, 0, tiled=True)]
where the time goes in v6:
time: 112 us; the launch traced here: 110 us
  blocking collectives  95.1 us (85%)
  Pallas kernels  13.9 us (12%)
    all_to_all x2, blocking collectives, local(): sums = lax.all_to_all(sums, 'tgt', 0, 0, tiled=True)  49.9 us
    all_to_all x1, blocking collectives, local(): lse = lax.all_to_all(lse, 'tgt', 0, 0, tiled=True)  26.1 us
    all_to_all x1, blocking collectives, local(): lse = lax.all_to_all(lse, 'src', 0, 0, tiled=True)  19.1 us
    pallas_call x5, Pallas kernels, call(): pl.pallas_call(kernel, out_shape=out_shape, in_specs=specs, out_specs=jax...  13.9 us

profile of v6, /device:TPU:1, one launch (start us, length us, event | category | flops | bytes accessed | tf_op | source)
XLA Modules:
  0.0 109.7 jit_solution(18116930018864594851)
XLA Ops:
  0.6 0.0 copy-start
  0.6 4.5 %shard_map.102 = (f32[16,512,512]{2,1,0:T(8,128)S(1)}, f32[32,8,128]{2,1,0:T(8,128)S(1)}, s32[1,128]{1,0:T(1,128)S(1)}, f32[8,128]{1,0:T(8,128)S(1)}, f32[32,128]{1,0:T(8,128)S(1)}) custom-call(s32[2]{0:T(128)} %count_hbm.1, s32[2,128]{1,0:T(2,128)} %ids_hbm.1, bf16[300,1024]{1,0:T(8,128)(2,1)} %bitcast.11, bf16[300,4096]{1,0:T(8,128)(2,1)} %bitcast.9, ...), custom_call_target="tpu_custom_call" | custom-call | tf_op jit(solution)/shard_map/pallas_call | solution.py:391
  5.1 26.1 %all_to_all.20.lse_ref = f32[32,8,128]{2,1,0:T(8,128)S(1)} all-to-all(f32[32,8,128]{2,1,0:T(8,128)S(1)} %get-tuple-element.18), channel_id=1, replica_groups=mesh['tgt'=32,'src'=16] {'tgt'}, dimensions={0} | all-to-all | bytes 262144 | tf_op jit(solution)/shard_map/all_to_all | solution.py:503
  31.2 1.4 %shard_map.103 = (f32[8,128]{1,0:T(8,128)}, f32[1024,128]{1,0:T(8,128)S(1)}, f32[16,32,128]{2,1,0:T(8,128)S(1)}) custom-call(s32[1,128]{1,0:T(1,128)S(1)} %get-tuple-element.16.list_ref, f32[16,512,512]{2,1,0:T(8,128)S(1)} %get-tuple-element.17.scores_ref, f32[32,8,128]{2,1,0:T(8,128)S(1)} %all_to_all.20.lse_ref, f32[8,128]{1,0:T(8,128)S(1)} %get-tuple-element.19.log_ref), custom_call_target="tpu_custom_call" | custom-call | tf_op jit(solution)/shard_map/pallas_call | solution.py:391
  32.6 19.1 %all_to_all.21.lse_ref = f32[16,32,128]{2,1,0:T(8,128)S(1)} all-to-all(f32[16,32,128]{2,1,0:T(8,128)S(1)} %get-tuple-element.21), channel_id=1, replica_groups=mesh['tgt'=32,'src'=16] {'src'}, dimensions={0} | all-to-all | bytes 524288 | tf_op jit(solution)/shard_map/all_to_all | solution.py:505
  51.7 0.0 copy-done
  51.7 6.7 %shard_map.104 = (f32[32,128]{1,0:T(8,128)}, bf16[32,80,128]{2,1,0:T(8,128)(2,1)S(1)}) custom-call(s32[1,128]{1,0:T(1,128)S(1)} %get-tuple-element.16.list_ref, f32[16,512,512]{2,1,0:T(8,128)S(1)} %get-tuple-element.17.scores_ref, bf16[300,4096]{1,0:T(8,128)(2,1)S(1)} %bitcast.10, f32[16,32,128]{2,1,0:T(8,128)S(1)} %all_to_all.21.lse_ref, ...), custom_call_target="tpu_custom_call" | custom-call | tf_op jit(solution)/shard_map/pallas_call | solution.py:391
  58.4 26.4 %all_to_all.22.in_ref = bf16[32,80,128]{2,1,0:T(8,128)(2,1)S(1)} all-to-all(bf16[32,80,128]{2,1,0:T(8,128)(2,1)S(1)} %get-tuple-element.25), channel_id=1, replica_groups=mesh['tgt'=32,'src'=16] {'tgt'}, dimensions={0} | all-to-all | bytes 1310720 | tf_op jit(solution)/shard_map/all_to_all | solution.py:507
  84.8 0.2 shard_map.105
  85.0 23.6 %all_to_all.23.in_ref = bf16[32,80,128]{2,1,0:T(8,128)(2,1)S(1)} all-to-all(bf16[32,80,128]{2,1,0:T(8,128)(2,1)S(1)} %shard_map.105), channel_id=1, replica_groups=mesh['tgt'=32,'src'=16] {'tgt'}, dimensions={0} | all-to-all | bytes 1310720 | tf_op jit(solution)/shard_map/all_to_all | solution.py:516
  108.6 1.1 shard_map.106
Async XLA Ops:
  0.6 51.1 %copy-start = (bf16[4096,300]{0,1:T(8,128)(2,1)S(1)}, bf16[4096,300]{0,1:T(8,128)(2,1)}, u32[]{:S(2)}) copy-start(bf16[4096,300]{0,1:T(8,128)(2,1)} %param.8) | copy-start | bytes 7372804

commit v7 on v6

--- a/solution.py
+++ b/solution.py
@@ -6,6 +6,7 @@
 from jax import lax
 from jax.experimental import pallas as pl
 from jax.experimental.pallas import tpu as pltpu
+from jax.sharding import Mesh
 from jax.sharding import PartitionSpec as P
 
 BLOCK = 512
@@ -24,6 +25,8 @@
 GROUPS = 4
 CHUNK = 80
 NT = (((1,), (1,)), ((), ()))
+TGT = ("z", "x")
+TURNED = ("x", "z")
 F32 = jnp.float32
 BF16 = jnp.bfloat16
 
@@ -84,7 +87,7 @@
 
 
 def my_place():
-    return lax.axis_index("tgt").astype(jnp.int32)
+    return lax.axis_index(TGT).astype(jnp.int32)
 
 
 def block_of(index):
@@ -491,7 +494,7 @@
 def local(src_emb, tgt_emb, g_init, log_src, log_tgt, cand_ids, cand_count):
     s_rows, width = src_emb.shape
     t_cols = tgt_emb.shape[0]
-    n_tgt, n_src = lax.axis_size("tgt"), lax.axis_size("src")
+    n_tgt, n_src = lax.axis_size(TGT), lax.axis_size("src")
     src_t, tgt_t = src_emb.T, tgt_emb.T
     s_tile = (s_rows // LANES, LANES)
     t_tile = (t_cols // LANES, LANES)
@@ -500,11 +503,11 @@
         cand_count, cand_ids, src_t, tgt_t, g_init.reshape(1, t_cols),
         log_src.reshape(s_tile), log_tgt.reshape(t_tile), n_tgt,
     )
-    lse = lax.all_to_all(lse, "tgt", 0, 0, tiled=True)
+    lse = lax.all_to_all(lse, TURNED, 0, 0, tiled=True)
     f, fcol, lse = run_cols(order, scores, lse, log_src, n_src, t_cols)
     lse = lax.all_to_all(lse, "src", 0, 0, tiled=True)
     c, sums = run_map(order, scores, tgt_t, lse, log_tgt, fcol, n_tgt)
-    sums = lax.all_to_all(sums, "tgt", 0, 0, tiled=True)
+    sums = lax.all_to_all(sums, TURNED, 0, 0, tiled=True)
     part, chunk = width // GROUPS, sums.shape[2]
     sums = call(
         functools.partial(merge_kernel, part),
@@ -513,7 +516,7 @@
         [VMEM],
         sums,
     )
-    sums = lax.all_to_all(sums, "tgt", 0, 0, tiled=True)
+    sums = lax.all_to_all(sums, TURNED, 0, 0, tiled=True)
     mapped, mass = call(
         functools.partial(final_kernel, part),
         (jax.ShapeDtypeStruct((width, s_rows), BF16), jax.ShapeDtypeStruct(s_tile, F32)),
@@ -525,18 +528,20 @@
 
 
 def solution(mesh):
+    across = min(4, mesh.shape["tgt"])
+    parts = mesh.devices.reshape(mesh.shape["tgt"] // across, across, mesh.shape["src"])
     return jax.shard_map(
         local,
-        mesh=mesh,
+        mesh=Mesh(parts, (*TGT, "src")),
         in_specs=(
             P("src", None),
-            P("tgt", None),
-            P("tgt"),
+            P(TGT, None),
+            P(TGT),
             P("src"),
-            P("tgt"),
+            P(TGT),
             P("src", None),
             P("src"),
         ),
-        out_specs=(P("src"), P("tgt"), P("src", None), P("src")),
+        out_specs=(P("src"), P(TGT), P("src", None), P("src")),
         check_vma=False,
     )

time: 112 us -> 110 us (0.982)
  blocking collectives: 95.1 us -> 90.7 us
  Pallas kernels: 13.9 us -> 17.1 us
    all_to_all x3, blocking collectives: 76 us -> 70.2 us  [the longest x2 47 us: local(): sums = lax.all_to_all(sums, TURNED, 0, 0, tiled=True)]
    pallas_call x5, Pallas kernels: 13.9 us -> 17.1 us  [call(): pl.pallas_call(kernel, out_shape=out_shape, in_specs=specs, out_specs=jax...]
    all_to_all x1, blocking collectives: 19.1 us -> 20.5 us  [local(): lse = lax.all_to_all(lse, 'src', 0, 0, tiled=True)]
where the time goes in v7:
time: 110 us; the launch traced here: 108 us
  blocking collectives  90.7 us (82%)
  Pallas kernels  17.1 us (16%)
    all_to_all x2, blocking collectives, local(): sums = lax.all_to_all(sums, TURNED, 0, 0, tiled=True)  47 us
    all_to_all x1, blocking collectives, local(): lse = lax.all_to_all(lse, TURNED, 0, 0, tiled=True)  23.2 us
    all_to_all x1, blocking collectives, local(): lse = lax.all_to_all(lse, 'src', 0, 0, tiled=True)  20.5 us
    pallas_call x5, Pallas kernels, call(): pl.pallas_call(kernel, out_shape=out_shape, in_specs=specs, out_specs=jax...  17.1 us

profile of v7, /device:TPU:1, one launch (start us, length us, event | category | flops | bytes accessed | tf_op | source)
XLA Modules:
  0.0 108.5 jit_solution(3776911952615939531)
XLA Ops:
  0.6 0.0 copy-start
  0.6 5.3 %shard_map.102 = (f32[16,512,512]{2,1,0:T(8,128)S(1)}, f32[32,8,128]{2,1,0:T(8,128)S(1)}, s32[1,128]{1,0:T(1,128)S(1)}, f32[8,128]{1,0:T(8,128)S(1)}, f32[32,128]{1,0:T(8,128)S(1)}) custom-call(s32[2]{0:T(128)} %count_hbm.1, s32[2,128]{1,0:T(2,128)} %ids_hbm.1, bf16[300,1024]{1,0:T(8,128)(2,1)} %bitcast.11, bf16[300,4096]{1,0:T(8,128)(2,1)} %bitcast.9, ...), custom_call_target="tpu_custom_call" | custom-call | tf_op jit(solution)/shard_map/pallas_call | solution.py:394
  5.9 23.2 %all_to_all.20.lse_ref = f32[32,8,128]{2,1,0:T(8,128)S(1)} all-to-all(f32[32,8,128]{2,1,0:T(8,128)S(1)} %get-tuple-element.18), channel_id=1, replica_groups=mesh['z'=8,'x'=4,'src'=16] {'x','z'}, dimensions={0} | all-to-all | bytes 262144 | tf_op jit(solution)/shard_map/all_to_all | solution.py:506
  29.1 1.7 %shard_map.103 = (f32[8,128]{1,0:T(8,128)}, f32[1024,128]{1,0:T(8,128)S(1)}, f32[16,32,128]{2,1,0:T(8,128)S(1)}) custom-call(s32[1,128]{1,0:T(1,128)S(1)} %get-tuple-element.16.list_ref, f32[16,512,512]{2,1,0:T(8,128)S(1)} %get-tuple-element.17.scores_ref, f32[32,8,128]{2,1,0:T(8,128)S(1)} %all_to_all.20.lse_ref, f32[8,128]{1,0:T(8,128)S(1)} %get-tuple-element.19.log_ref), custom_call_target="tpu_custom_call" | custom-call | tf_op jit(solution)/shard_map/pallas_call | solution.py:394
  30.8 20.5 %all_to_all.21.lse_ref = f32[16,32,128]{2,1,0:T(8,128)S(1)} all-to-all(f32[16,32,128]{2,1,0:T(8,128)S(1)} %get-tuple-element.21), channel_id=1, replica_groups=mesh['z'=8,'x'=4,'src'=16] {'src'}, dimensions={0} | all-to-all | bytes 524288 | tf_op jit(solution)/shard_map/all_to_all | solution.py:508
  51.3 0.0 copy-done
  51.3 8.8 %shard_map.104 = (f32[32,128]{1,0:T(8,128)}, bf16[32,80,128]{2,1,0:T(8,128)(2,1)S(1)}) custom-call(s32[1,128]{1,0:T(1,128)S(1)} %get-tuple-element.16.list_ref, f32[16,512,512]{2,1,0:T(8,128)S(1)} %get-tuple-element.17.scores_ref, bf16[300,4096]{1,0:T(8,128)(2,1)S(1)} %bitcast.10, f32[16,32,128]{2,1,0:T(8,128)S(1)} %all_to_all.21.lse_ref, ...), custom_call_target="tpu_custom_call" | custom-call | tf_op jit(solution)/shard_map/pallas_call | solution.py:394
  60.2 24.5 %all_to_all.22.in_ref = bf16[32,80,128]{2,1,0:T(8,128)(2,1)S(1)} all-to-all(bf16[32,80,128]{2,1,0:T(8,128)(2,1)S(1)} %get-tuple-element.25), channel_id=1, replica_groups=mesh['z'=8,'x'=4,'src'=16] {'x','z'}, dimensions={0} | all-to-all | bytes 1310720 | tf_op jit(solution)/shard_map/all_to_all | solution.py:510
  84.7 0.2 shard_map.105
  84.9 22.4 %all_to_all.23.in_ref = bf16[32,80,128]{2,1,0:T(8,128)(2,1)S(1)} all-to-all(bf16[32,80,128]{2,1,0:T(8,128)(2,1)S(1)} %shard_map.105), channel_id=1, replica_groups=mesh['z'=8,'x'=4,'src'=16] {'x','z'}, dimensions={0} | all-to-all | bytes 1310720 | tf_op jit(solution)/shard_map/all_to_all | solution.py:519
  107.4 1.1 shard_map.106
Async XLA Ops:
  0.6 50.7 %copy-start = (bf16[4096,300]{0,1:T(8,128)(2,1)S(1)}, bf16[4096,300]{0,1:T(8,128)(2,1)}, u32[]{:S(2)}) copy-start(bf16[4096,300]{0,1:T(8,128)(2,1)} %param.8) | copy-start | bytes 7372804

commit v8 on v6

--- a/solution.py
+++ b/solution.py
@@ -69,7 +69,13 @@
             use(1, tile(i + 1), start)
         return carry
 
-    lax.fori_loop(0, (order_ref[0, COUNT] + 1) // 2, step, 0)
+    count = order_ref[0, COUNT]
+    lax.fori_loop(0, count // 2, step, 0)
+
+    @pl.when(count % 2 == 1)
+    def _():
+        for start in starts:
+            use(0, tile(count - 1), start)
 
 
 def each(order_ref, columns, use):
@@ -80,7 +86,12 @@
         use(tile(2 * k + 1))
         return carry
 
-    lax.fori_loop(0, (order_ref[0, COUNT] + 1) // 2, step, 0)
+    count = order_ref[0, COUNT]
+    lax.fori_loop(0, count // 2, step, 0)
+
+    @pl.when(count % 2 == 1)
+    def _():
+        use(tile(count - 1))
 
 
 def my_place():

time: 112 us -> 110 us (0.982)
  the two profiles are of different devices: /device:TPU:1 before, /device:TPU:2 now
where the time goes in v8:
time: 110 us; the launch traced here: 109 us
  blocking collectives  92.9 us (84%)
  Pallas kernels  15.2 us (14%)
    all_to_all x2, blocking collectives, local(): sums = lax.all_to_all(sums, 'tgt', 0, 0, tiled=True)  50.6 us
    all_to_all x1, blocking collectives, local(): lse = lax.all_to_all(lse, 'tgt', 0, 0, tiled=True)  22.9 us
    all_to_all x1, blocking collectives, local(): lse = lax.all_to_all(lse, 'src', 0, 0, tiled=True)  19.3 us
    pallas_call x5, Pallas kernels, call(): pl.pallas_call(kernel, out_shape=out_shape, in_specs=specs, out_specs=jax...  15.2 us

profile of v8, /device:TPU:2, one launch (start us, length us, event | category | flops | bytes accessed | tf_op | source)
XLA Modules:
  0.0 108.8 jit_solution(6980710517290740326)
XLA Ops:
  0.6 0.0 copy-start
  0.6 4.7 %shard_map.102 = (f32[16,512,512]{2,1,0:T(8,128)S(1)}, f32[32,8,128]{2,1,0:T(8,128)S(1)}, s32[1,128]{1,0:T(1,128)S(1)}, f32[8,128]{1,0:T(8,128)S(1)}, f32[32,128]{1,0:T(8,128)S(1)}) custom-call(s32[2]{0:T(128)} %count_hbm.1, s32[2,128]{1,0:T(2,128)} %ids_hbm.1, bf16[300,1024]{1,0:T(8,128)(2,1)} %bitcast.11, bf16[300,4096]{1,0:T(8,128)(2,1)} %bitcast.9, ...), custom_call_target="tpu_custom_call" | custom-call | tf_op jit(solution)/shard_map/pallas_call | solution.py:402
  5.4 22.9 %all_to_all.20.lse_ref = f32[32,8,128]{2,1,0:T(8,128)S(1)} all-to-all(f32[32,8,128]{2,1,0:T(8,128)S(1)} %get-tuple-element.18), channel_id=1, replica_groups=mesh['tgt'=32,'src'=16] {'tgt'}, dimensions={0} | all-to-all | bytes 262144 | tf_op jit(solution)/shard_map/all_to_all | solution.py:514
  28.3 1.6 %shard_map.103 = (f32[8,128]{1,0:T(8,128)}, f32[1024,128]{1,0:T(8,128)S(1)}, f32[16,32,128]{2,1,0:T(8,128)S(1)}) custom-call(s32[1,128]{1,0:T(1,128)S(1)} %get-tuple-element.16.list_ref, f32[16,512,512]{2,1,0:T(8,128)S(1)} %get-tuple-element.17.scores_ref, f32[32,8,128]{2,1,0:T(8,128)S(1)} %all_to_all.20.lse_ref, f32[8,128]{1,0:T(8,128)S(1)} %get-tuple-element.19.log_ref), custom_call_target="tpu_custom_call" | custom-call | tf_op jit(solution)/shard_map/pallas_call | solution.py:402
  29.9 19.3 %all_to_all.21.lse_ref = f32[16,32,128]{2,1,0:T(8,128)S(1)} all-to-all(f32[16,32,128]{2,1,0:T(8,128)S(1)} %get-tuple-element.21), channel_id=1, replica_groups=mesh['tgt'=32,'src'=16] {'src'}, dimensions={0} | all-to-all | bytes 524288 | tf_op jit(solution)/shard_map/all_to_all | solution.py:516
  49.2 0.0 copy-done
  49.2 7.6 %shard_map.104 = (f32[32,128]{1,0:T(8,128)}, bf16[32,80,128]{2,1,0:T(8,128)(2,1)S(1)}) custom-call(s32[1,128]{1,0:T(1,128)S(1)} %get-tuple-element.16.list_ref, f32[16,512,512]{2,1,0:T(8,128)S(1)} %get-tuple-element.17.scores_ref, bf16[300,4096]{1,0:T(8,128)(2,1)S(1)} %bitcast.10, f32[16,32,128]{2,1,0:T(8,128)S(1)} %all_to_all.21.lse_ref, ...), custom_call_target="tpu_custom_call" | custom-call | tf_op jit(solution)/shard_map/pallas_call | solution.py:402
  56.8 26.7 %all_to_all.22.in_ref = bf16[32,80,128]{2,1,0:T(8,128)(2,1)S(1)} all-to-all(bf16[32,80,128]{2,1,0:T(8,128)(2,1)S(1)} %get-tuple-element.25), channel_id=1, replica_groups=mesh['tgt'=32,'src'=16] {'tgt'}, dimensions={0} | all-to-all | bytes 1310720 | tf_op jit(solution)/shard_map/all_to_all | solution.py:518
  83.5 0.2 shard_map.105
  83.8 23.9 %all_to_all.23.in_ref = bf16[32,80,128]{2,1,0:T(8,128)(2,1)S(1)} all-to-all(bf16[32,80,128]{2,1,0:T(8,128)(2,1)S(1)} %shard_map.105), channel_id=1, replica_groups=mesh['tgt'=32,'src'=16] {'tgt'}, dimensions={0} | all-to-all | bytes 1310720 | tf_op jit(solution)/shard_map/all_to_all | solution.py:527
  107.7 1.1 shard_map.106
Async XLA Ops:
  0.6 48.6 %copy-start = (bf16[4096,300]{0,1:T(8,128)(2,1)S(1)}, bf16[4096,300]{0,1:T(8,128)(2,1)}, u32[]{:S(2)}) copy-start(bf16[4096,300]{0,1:T(8,128)(2,1)} %param.8) | copy-start | bytes 7372804
